TPU v7x, 512 devices: a whole 4x8x8 slice. The times are simulated.
512 devices in a mesh: grp: 4 (over x), seq: 16 (over y, core), tp: 8 (over z).
Axes of the slice: x: 4, y: 8, z: 8, core: 2. Of those that a mesh axis runs over, the one named last changes fastest.
Arguments:
- byte_states: bfloat16 [4, 4096, 1024], P('grp', 'seq', 'tp'), may hold values from -6 to 6
- patch_map: int32 [4, 4096], P('grp', 'seq'), may hold values from 0 to 63, as said below
- lift_weight: bfloat16 [1024, 4096], P('tp'), may hold values from -0.1875 to 0.1875
- gate_weight: bfloat16 [4096, 8192], P('seq', ('grp', 'tp')), may hold values from -0.09375 to 0.09375
- up_weight: bfloat16 [4096, 8192], P('seq', ('grp', 'tp')), may hold values from -0.09375 to 0.09375
- down_weight: bfloat16 [8192, 4096], P(('grp', 'tp'), 'seq'), may hold values from -0.0625 to 0.0625
- return_weight: bfloat16 [4096, 1024], P(None, 'tp'), may hold values from -0.09375 to 0.09375
Outputs:
- byte_output: bfloat16 [4, 4096, 1024], P('grp', 'seq', 'tp')
Inputs may be any that keep to these rules, and one draw needn't show every extreme that they name: `patch_map`: within each block of 256 bytes the values never fall, start at 0 and take every value from 0 to n - 1, with n one of 64, 32, 16, 8; in every sequence some block has n = 64.
All inputs are finite; a program needn't handle non-finite values.
Results may differ from a plain program's by a relative error of at most 0.025.
Values may be sent and summed in bfloat16 or wider, within the bound.
A program may use at most 64 MiB of HBM per device.

v0:
```python
import jax
import jax.numpy as jnp
from jax import lax
from jax.sharding import PartitionSpec as P

DL = 1024
NMAX = 64


epsilon = 1e-05


def on_device(
    byte_states, patch_map, lift_weight, gate_weight, up_weight, down_weight, return_weight
):
    states = byte_states[0]
    slot_ids = patch_map[0]
    onehot = (slot_ids[:, None] == jnp.arange(NMAX, dtype=jnp.int32)[None, :]).astype(jnp.bfloat16)
    counts = jnp.sum(onehot.astype(jnp.float32), axis=0)
    byte_sums = lax.dot_general(
        onehot, states, (((0,), (0,)), ((), ())), preferred_element_type=jnp.float32
    )
    pooled = (byte_sums / jnp.maximum(counts, 1.0)[:, None]).astype(jnp.bfloat16)
    group_id = lax.axis_index("grp")
    lifted = jnp.dot(pooled, lift_weight, preferred_element_type=jnp.float32)
    lifted = lax.psum(lifted.astype(jnp.bfloat16), "tp")
    gathered = lax.all_gather(lifted, "grp", axis=0, tiled=True)
    widened = gathered.astype(jnp.float32)
    normed = (
        widened * lax.rsqrt(jnp.mean(widened * widened, axis=1, keepdims=True) + epsilon)
    ).astype(jnp.bfloat16)
    gate_act = jnp.dot(
        normed,
        lax.all_gather(gate_weight, "seq", axis=0, tiled=True),
        preferred_element_type=jnp.float32,
    )
    up_act = jnp.dot(
        normed,
        lax.all_gather(up_weight, "seq", axis=0, tiled=True),
        preferred_element_type=jnp.float32,
    )
    hidden = (jax.nn.silu(gate_act) * up_act).astype(jnp.bfloat16)
    partial_value = jnp.dot(
        hidden,
        lax.all_gather(down_weight, "seq", axis=1, tiled=True),
        preferred_element_type=jnp.float32,
    )
    latent_delta = lax.psum_scatter(
        partial_value.astype(jnp.bfloat16), ("grp", "tp"), scatter_dimension=0, tiled=True
    ).astype(jnp.float32)
    block_rows = latent_delta.shape[0]
    first_row = group_id * NMAX + lax.axis_index("tp") * block_rows
    own_rows = lax.dynamic_slice_in_dim(widened, first_row, block_rows, 0)
    patch_share = (own_rows + latent_delta).astype(jnp.bfloat16)
    patch_out = lax.all_gather(patch_share, "tp", axis=0, tiled=True)
    returned = jnp.dot(patch_out, return_weight, preferred_element_type=jnp.float32).astype(
        jnp.bfloat16
    )
    spread = jnp.dot(onehot, returned, preferred_element_type=jnp.float32)
    mixed_rows = states.astype(jnp.float32) + spread
    square_sum = lax.psum(jnp.sum(mixed_rows * mixed_rows, axis=1), "tp")
    scaled = mixed_rows * lax.rsqrt(square_sum / DL + epsilon)[:, None]
    return scaled.astype(jnp.bfloat16)[None]


def solution(mesh):
    placed = (
        P("grp", "seq", "tp"),
        P("grp", "seq"),
        P("tp", None),
        P("seq", ("grp", "tp")),
        P("seq", ("grp", "tp")),
        P(("grp", "tp"), "seq"),
        P(None, "tp"),
    )
    return jax.shard_map(
        on_device, mesh=mesh, in_specs=placed, out_specs=P("grp", "seq", "tp"), check_vma=False
    )
```

profile of v0, /device:TPU:8, one launch (start us, length us, event | category | flops | bytes accessed | tf_op | source)
XLA Modules:
  0.0 542.4 jit_solution(10833458891368314139)
XLA Ops:
  6.5 0.0 copy-start
  6.5 0.0 all-reduce.2.cloned.1.call-start
  6.5 0.9 convert_reduce_fusion
  7.4 0.3 copy-done
  7.8 2.1 convolution_convert_fusion.1
  9.8 0.0 all-reduce.2.cloned.1.call-update
  9.9 0.0 all-gather.5.cloned.1.call-start
  9.9 84.3 %all-reduce.2.cloned.1.call-done = bf16[64,4096]{1,0:T(8,128)(2,1)} async-done(((bf16[64,4096]{1,0:T(8,128)(2,1)}), bf16[64,4096]{1,0:T(8,128)(2,1)}) %all-reduce.2.cloned.1.call-update) | async-done | bytes 524304 | tf_op jit(solution)/shard_map/psum | solution.py:26
  94.3 0.0 all-gather.5.cloned.1.call-update
  94.3 0.0 all-gather.7.cloned.1.call-start
  94.3 0.7 all-gather.7.cloned.1.call-update
  95.0 0.0 all-gather.11.cloned.1.call-start
  95.1 0.5 all-gather.11.cloned.1.call-update
  95.6 0.0 all-gather.9.cloned.1.call-start
  95.6 0.5 all-gather.9.cloned.1.call-update
  96.2 0.0 reduce-scatter.2.cloned.1.call-start
  96.2 34.5 %all-gather.5.cloned.1.call-done = bf16[256,4096]{1,0:T(8,128)(2,1)} async-done(((bf16[64,4096]{1,0:T(8,128)(2,1)}), bf16[256,4096]{1,0:T(8,128)(2,1)}) %all-gather.5.cloned.1.call-update) | async-done | bytes 2097168 | tf_op jit(solution)/shard_map/all_gather | solution.py:27
  130.7 0.0 copy-start.1
  130.7 2.2 multiply_reduce_fusion
  133.0 41.8 %all-gather.7.cloned.1.call-done = bf16[4096,256]{1,0:T(8,128)(2,1)} async-done(((bf16[256,256]{1,0:T(8,128)(2,1)}), bf16[4096,256]{1,0:T(8,128)(2,1)}) %all-gather.7.cloned.1.call-update) | async-done | bytes 2097168 | tf_op jit(solution)/shard_map/all_gather | solution.py:34
  174.8 0.0 copy-done.1
  174.8 2.3 fusion.2
  177.1 42.4 %all-gather.11.cloned.1.call-done = bf16[256,4096]{1,0:T(8,128)(2,1)} async-done(((bf16[256,256]{1,0:T(8,128)(2,1)}), bf16[256,4096]{1,0:T(8,128)(2,1)}) %all-gather.11.cloned.1.call-update) | async-done | bytes 2097168 | tf_op jit(solution)/shard_map/all_gather | solution.py:45
  219.5 43.3 %all-gather.9.cloned.1.call-done = bf16[4096,256]{1,0:T(8,128)(2,1)} async-done(((bf16[256,256]{1,0:T(8,128)(2,1)}), bf16[4096,256]{1,0:T(8,128)(2,1)}) %all-gather.9.cloned.1.call-update) | async-done | bytes 2097168 | tf_op jit(solution)/shard_map/all_gather | solution.py:39
  262.8 6.0 %convolution_convert_fusion = bf16[256,4096]{1,0:T(8,128)(2,1)} fusion(bf16[256,4096]{1,0:T(8,128)(2,1)} %all-gather.11.cloned.1.call-done, bf16[4096,256]{1,0:T(8,128)(2,1)} %all-gather.9.cloned.1.call-done, f32[256]{0:T(256)S(1)} %add_rsqrt_fusion.1, bf16[256,4096]{1,0:T(8,128)(2,1)S(1)} %copy-done.1, f32[256,256]{1,0:T(8,128)S(1)} %fusion.2), kind=kOutput, calls=%fused_computation | convolution fusion | flops 1078329344 | bytes 8651776 | tf_op jit(solution)/shard_map/dot_general | solution.py:43
  268.7 0.0 copy-start.2
  268.7 0.0 reduce-scatter.2.cloned.1.call-update
  268.8 0.8 copy-done.2
  269.6 0.1 copy.10
  269.7 0.0 copy-start.3
  269.7 2.4 convert_element_type.44
  272.1 218.4 %reduce-scatter.2.cloned.1.call-done = bf16[8,4096]{1,0:T(8,128)(2,1)} async-done(((bf16[256,4096]{1,0:T(8,128)(2,1)}), bf16[8,4096]{1,0:T(8,128)(2,1)}) %reduce-scatter.2.cloned.1.call-update) | async-done | bytes 65552 | tf_op jit(solution)/shard_map/reduce_scatter | solution.py:48
  490.5 1.0 add_convert_fusion
  491.5 25.3 %all_gather.19 = bf16[64,4096]{1,0:T(8,128)(2,1)S(1)} all-gather(bf16[8,4096]{1,0:T(8,128)(2,1)S(1)} %add_convert_fusion), channel_id=1, replica_groups=mesh['grp'=4,'seq'=16,'tp'=8] {'tp'}, dimensions={0}, use_global_device_ids=true | all-gather | bytes 589824 | tf_op jit(solution)/shard_map/all_gather | solution.py:55
  516.9 0.0 copy-done.3
  516.9 1.8 multiply_reduce_fusion.1
  518.6 16.1 %psum.15 = f32[256]{0:T(256)S(1)} all-reduce(f32[256]{0:T(256)S(1)} %get-tuple-element.5), channel_id=1, replica_groups=mesh['grp'=4,'seq'=16,'tp'=8] {'tp'}, use_global_device_ids=true, to_apply=%region_5.6 | all-reduce | flops 256 | bytes 2048 | tf_op jit(solution)/shard_map/psum | solution.py:61
  534.8 0.7 copy.11
  (4 shorter events, 0.0 us)
Async XLA Ops:
  6.5 1.2 copy-start
  6.5 87.7 %all-reduce.2.cloned.1.call-start = ((), (), s32[]{:S(2)}) async-start(), calls=%async_computation.1 | async-start | bytes 1048576 | tf_op jit(solution)/shard_map/psum | solution.py:26
  9.9 120.9 %all-gather.5.cloned.1.call-start = ((), (), s32[]{:S(2)}) async-start(), calls=%async_computation.2 | async-start | bytes 2621440 | tf_op jit(solution)/shard_map/all_gather | solution.py:27
  94.3 80.5 %all-gather.7.cloned.1.call-start = ((), (), s32[]{:S(2)}) async-start(), calls=%async_computation.3 | async-start | bytes 2228224 | tf_op jit(solution)/shard_map/all_gather | solution.py:34
  95.0 124.5 %all-gather.11.cloned.1.call-start = ((), (), s32[]{:S(2)}) async-start(), calls=%async_computation.5 | async-start | bytes 2228224 | tf_op jit(solution)/shard_map/all_gather | solution.py:45
  95.6 167.2 %all-gather.9.cloned.1.call-start = ((), (), s32[]{:S(2)}) async-start(), calls=%async_computation.4 | async-start | bytes 2228224 | tf_op jit(solution)/shard_map/all_gather | solution.py:39
  96.2 394.4 %reduce-scatter.2.cloned.1.call-start = ((), (), s32[]{:S(2)}) async-start(), calls=%async_computation.6 | async-start | bytes 2162688 | tf_op jit(solution)/shard_map/reduce_scatter | solution.py:48
  130.7 44.0 %copy-start.1 = (bf16[256,4096]{1,0:T(8,128)(2,1)S(1)}, bf16[256,4096]{1,0:T(8,128)(2,1)}, u32[]{:S(2)}) copy-start(bf16[256,4096]{1,0:T(8,128)(2,1)} %all-gather.5.cloned.1.call-done) | copy-start | bytes 6291460
  268.7 0.8 copy-start.2
  269.7 247.2 %copy-start.3 = (s32[1,256]{1,0:T(1,128)S(1)}, s32[1,256]{1,0:T(1,128)}, u32[]{:S(2)}) copy-start(s32[1,256]{1,0:T(1,128)} %param.8) | copy-start | bytes 3076
Sparse Core Ops, SparseCore 0:
  10.0 84.2 all-reduce.1
  96.6 34.1 all-gather.4
  133.1 41.6 all-gather.6
  176.9 42.5 all-gather.10
  221.7 41.0 all-gather.8
  268.9 221.6 reduce-scatter.1
where the time goes:
time: 543 us; the launch traced here: 542 us
  waiting for transfers between devices  467 us (86%)
  blocking collectives  41.5 us (8%)
  between operations  13.5 us (2%)
  matrix products  12.1 us (2%)
  other arithmetic  6.52 us (1%)
    reduce_scatter x1, waiting for transfers between devices, on_device(): lax.psum_scatter(partial_value.astype(jnp.bfloat16), ('grp', 'tp'), scatt...  218 us
    psum x1, waiting for transfers between devices, on_device(): lifted = lax.psum(lifted.astype(jnp.bfloat16), 'tp')  84.3 us
    all_gather x1, waiting for transfers between devices, on_device(): lax.all_gather(up_weight, 'seq', axis=0, tiled=True)  43.3 us
    all_gather x1, waiting for transfers between devices, on_device(): lax.all_gather(down_weight, 'seq', axis=1, tiled=True)  42.4 us
    all_gather x1, waiting for transfers between devices, on_device(): lax.all_gather(gate_weight, 'seq', axis=0, tiled=True)  41.8 us
    all_gather x1, waiting for transfers between devices, on_device(): gathered = lax.all_gather(lifted, 'grp', axis=0, tiled=True)  34.5 us
    all_gather x1, blocking collectives, on_device(): patch_out = lax.all_gather(patch_share, 'tp', axis=0, tiled=True)  25.3 us
    psum x1, blocking collectives, on_device(): square_sum = lax.psum(jnp.sum(mixed_rows * mixed_rows, axis=1), 'tp')  16.1 us
  transfers between devices with their start and end apart: 6, of which 6 were waited for; matrix products, arithmetic and copies ran while one was open for 1% of the time, Pallas kernels for 0%

commit v1 on v0

v1 whole, which is shorter than its diff:
```python
import jax
import jax.numpy as jnp
from jax import lax
from jax.experimental import pallas as pl
from jax.experimental.pallas import tpu as pltpu
from jax.sharding import PartitionSpec as P

DL = 1024
NMAX = 64
EPS = 1e-05
MESH = pl.DeviceIdType.MESH
F32 = jnp.float32
BF16 = jnp.bfloat16
OUT_ORDER = (4, 3, 5, 2, 6, 1, 7, 0)
IN_ORDER = (0, 1, 7, 2, 6, 3, 5, 4)


def dot(a, b):
    return jnp.dot(a, b, preferred_element_type=F32)


def kernel(
    states_ref, map_ref, lift_hbm, gate_hbm, up_hbm, down_hbm, ret_hbm, out_ref,
    lift, weights, lift_out, lift_in, patch, acc, part, half_in, pair_out, pair_in,
    done_out, done_in, ret, back_out, back_in, sq_out, sq_in,
    load_sem, y_send, y_recv, sib_send, sib_recv, lift_send, lift_recv,
    zg_send, zg_recv, xg_send, xg_recv, ret_send, ret_recv, rsib_send, rsib_recv,
    h_send, h_recv, p_send, p_recv, d_send, d_recv, b_send, b_recv, q_send, q_recv,
):
    x = lax.axis_index("grp")
    s = lax.axis_index("seq")
    z = lax.axis_index("tp")
    y = s // 2
    c = s % 2
    xa = x + 1 - 2 * (x % 2)
    xb = 3 - x
    sib = 2 * y + 1 - c
    started = []

    def z_at(d):
        return (z + d + 8) % 8

    def slot(q):
        return 2 * ((y + q + 8) % 8) + c

    def remote(src, dst, ss, rs, device):
        return pltpu.make_async_remote_copy(
            src_ref=src, dst_ref=dst, send_sem=ss, recv_sem=rs,
            device_id=device, device_id_type=MESH,
        )

    def send(src, dst, ss, rs, device):
        copy = remote(src, dst, ss, rs, device)
        copy.start()
        started.append(copy)

    def arrived(ref, ss, rs, device):
        remote(ref, ref, ss, rs, device).wait_recv()

    loads = [
        pltpu.make_async_copy(gate_hbm, weights.at[s, 0], load_sem.at[0]),
        pltpu.make_async_copy(up_hbm, weights.at[s, 1], load_sem.at[1]),
        pltpu.make_async_copy(down_hbm, weights.at[s, 2], load_sem.at[2]),
        pltpu.make_async_copy(lift_hbm, lift, load_sem.at[3]),
        pltpu.make_async_copy(ret_hbm.at[pl.ds(z * 512, 512)], ret.at[0], load_sem.at[4]),
    ]
    for load in loads:
        load.start()
    barrier = pltpu.get_barrier_semaphore()
    partners = [{"seq": slot(1)}, {"seq": slot(-1)}, {"seq": sib}, {"grp": xa}, {"grp": xb}]
    partners += [{"tp": z_at(d)} for d in range(1, 8)]
    for partner in partners:
        pl.semaphore_signal(barrier, inc=1, device_id=partner, device_id_type=MESH)
    pl.semaphore_wait(barrier, len(partners))
    for load in loads[:3]:
        load.wait()

    def y_ref(q, st, way, hop):
        rows = pl.ds(0, 256) if hop < 3 else pl.ds(128 * way, 128)
        first, count = ((0, 2), (2, 1))[st]
        return weights.at[slot(q), pl.ds(first, count), rows]

    def y_go(way, hop, st):
        q = -hop if way == 0 else hop
        ref = y_ref(q, st, way, hop)
        send(ref, ref, y_send.at[way, hop, st], y_recv.at[way, hop, st],
             {"seq": slot(1 if way == 0 else -1)})

    def sib_go(q, st):
        ref = y_ref(q, st, 0, 0)
        k = q % 8
        send(ref, ref, sib_send.at[k, st], sib_recv.at[k, st], {"seq": sib})

    def y_start():
        for st in (0, 1):
            y_go(0, 0, st)
            y_go(1, 0, st)
            sib_go(0, st)

    def y_step(hop, st):
        for way in (0, 1):
            q = -(hop + 1) if way == 0 else hop + 1
            arrived(y_ref(q, st, way, hop), y_send.at[way, hop, st], y_recv.at[way, hop, st],
                    {"seq": slot(1)})
            if hop < 3:
                y_go(way, hop + 1, st)
                sib_go(q, st)
        if hop == 3:
            sib_go(4, st)

    def sib_wait(st):
        first, count = ((0, 2), (2, 1))[st]
        for k in range(8):
            ref = weights.at[2 * ((y + k) % 8) + 1 - c, pl.ds(first, count)]
            arrived(ref, sib_send.at[k, st], sib_recv.at[k, st], {"seq": sib})

    y_start()

    map_row = map_ref[...]
    onehot = (lax.broadcasted_iota(jnp.int32, (NMAX, 256), 0) == map_row).astype(F32)
    counts = jnp.sum(onehot, axis=1, keepdims=True)
    states = states_ref[...]
    sums = dot(onehot.astype(BF16), states)
    pooled = (sums / jnp.maximum(counts, 1.0)).astype(BF16)
    loads[3].wait()
    for k in range(8):
        lift_out[k] = dot(pooled, lift[:, 512 * k : 512 * (k + 1)]).astype(BF16)
    for d in (4, 3, 5, 2, 6, 1, 7):
        send(lift_out.at[z_at(d)], lift_in.at[d], lift_send.at[d], lift_recv.at[d],
             {"tp": z_at(d)})

    y_step(0, 0)
    y_step(0, 1)

    block = lift_out[z].astype(F32)
    for d in (1, 7, 2, 6, 3, 5, 4):
        arrived(lift_in.at[d], lift_send.at[d], lift_recv.at[d], {"tp": z_at(d)})
        block = block + lift_in[d].astype(F32)
    patch[0, 0] = block.astype(BF16)

    def zg_ref(e, way, hop):
        rows = pl.ds(0, 64) if hop < 3 else pl.ds(32 * way, 32)
        return patch.at[e, 0, rows]

    def zg_go(way, hop):
        e = hop if way == 0 else (8 - hop) % 8
        e2 = hop + 1 if way == 0 else 7 - hop
        send(zg_ref(e, way, hop), zg_ref(e2, way, hop), zg_send.at[way, hop],
             zg_recv.at[way, hop], {"tp": z_at(1 if way == 0 else -1)})

    def zg_wait(way, hop):
        e = hop + 1 if way == 0 else 7 - hop
        arrived(zg_ref(e, way, hop), zg_send.at[way, hop], zg_recv.at[way, hop],
                {"tp": z_at(1)})

    def first_second(i):
        return ((xa, 1), (xb, 3)) if i % 2 == 0 else ((xb, 3), (xa, 1))

    def xg_one(i):
        e = IN_ORDER[i]
        (n1, j1), _ = first_second(i)
        send(patch.at[e, 0], patch.at[e, j1], xg_send.at[e, 0], xg_recv.at[e, 0], {"grp": n1})

    def xg_two(i):
        e = IN_ORDER[i]
        (n1, j1), (n2, j2) = first_second(i)
        send(patch.at[e, 0], patch.at[e, j2], xg_send.at[e, 1], xg_recv.at[e, 1], {"grp": n2})
        arrived(patch.at[e, j1], xg_send.at[e, 0], xg_recv.at[e, 0], {"grp": n1})
        send(patch.at[e, j1], patch.at[e, 2], xg_send.at[e, 2], xg_recv.at[e, 2], {"grp": n2})

    def xg_wait(i):
        e = IN_ORDER[i]
        _, (n2, j2) = first_second(i)
        arrived(patch.at[e, j2], xg_send.at[e, 1], xg_recv.at[e, 1], {"grp": n2})
        arrived(patch.at[e, 2], xg_send.at[e, 2], xg_recv.at[e, 2], {"grp": n2})

    zg_go(0, 0)
    zg_go(1, 0)
    xg_one(0)
    y_step(1, 0)
    zg_wait(0, 0)
    zg_go(0, 1)
    xg_one(1)
    zg_wait(1, 0)
    zg_go(1, 1)
    xg_one(2)
    xg_two(0)
    y_step(1, 1)
    zg_wait(0, 1)
    zg_go(0, 2)
    xg_one(3)
    zg_wait(1, 1)
    zg_go(1, 2)
    xg_one(4)
    xg_two(1)
    xg_two(2)
    y_step(2, 0)
    zg_wait(0, 2)
    zg_go(0, 3)
    xg_one(5)
    zg_wait(1, 2)
    zg_go(1, 3)
    xg_one(6)
    xg_two(3)
    xg_two(4)
    y_step(2, 1)
    zg_wait(0, 3)
    zg_wait(1, 3)
    xg_one(7)

    half = pl.ds(256 * c, 256)
    other = pl.ds(256 * (1 - c), 256)
    for d in (4, 3, 5, 2, 6, 1, 7):
        send(ret_hbm.at[pl.ds(z_at(d) * 512 + 256 * c, 256)], ret.at[d, half],
             ret_send.at[d], ret_recv.at[d], {"tp": z_at(d)})

    xg_two(5)
    xg_two(6)
    y_step(3, 0)
    y_step(3, 1)
    xg_two(7)
    sib_wait(0)

    squares = jnp.zeros((256, 1), F32)
    for i in range(8):
        e = IN_ORDER[i]
        if i > 0:
            xg_wait(i)
        else:
            xg_wait(0)
        kb = z_at(-e)
        rows = patch[e].reshape(256, 512)
        wide = rows.astype(F32)
        squares = squares + jnp.sum(wide * wide, axis=1, keepdims=True)
        for a in (0, 1):
            w = weights[pl.ds(2 * kb, 2), a].reshape(512, 256)
            if i == 0:
                acc[a] = dot(rows, w)
            else:
                acc[a] += dot(rows, w)
    scale = lax.rsqrt(squares * (1.0 / 4096) + EPS)
    gate = acc[0] * scale
    up = acc[1] * scale
    hidden = (gate / (1.0 + jnp.exp(-gate)) * up).astype(BF16)

    sib_wait(1)

    def down_one(i):
        kb = z_at(OUT_ORDER[i])
        for n in (0, 1):
            val = dot(hidden, weights[2 * kb + n, 2]).astype(BF16)
            part[i, :, :, 256 * n : 256 * (n + 1)] = val.reshape(4, 64, 256)
        (n1, j1), _ = first_second(i)
        src = part.at[i, pl.ds(1 if j1 == 1 else 2, 2)]
        send(src, half_in.at[i], h_send.at[i], h_recv.at[i], {"grp": n1})

    def down_two(i):
        (n1, j1), (n2, j2) = first_second(i)
        arrived(half_in.at[i], h_send.at[i], h_recv.at[i], {"grp": n1})
        other_row = 1 if j1 == 1 else 0
        pair_out[i] = (part[i, j2].astype(F32) + half_in[i, other_row].astype(F32)).astype(BF16)
        send(pair_out.at[i], pair_in.at[i], p_send.at[i], p_recv.at[i], {"grp": n2})

    def down_three(i):
        (n1, j1), (n2, j2) = first_second(i)
        arrived(pair_in.at[i], p_send.at[i], p_recv.at[i], {"grp": n2})
        own_row = 0 if j1 == 1 else 1
        total = (
            part[i, 0].astype(F32) + half_in[i, own_row].astype(F32) + pair_in[i].astype(F32)
        )
        d = OUT_ORDER[i]
        if d == 0:
            return total
        done_out[i] = total.astype(BF16)
        send(done_out.at[i], done_in.at[d], d_send.at[d], d_recv.at[d], {"tp": z_at(d)})
        return None

    for i in range(8):
        down_one(i)
    delta = None
    for i in range(9):
        if i < 8:
            down_two(i)
        if i > 0:
            delta = down_three(i - 1)

    loads[4].wait()
    for d in range(1, 8):
        arrived(ret.at[d, half], ret_send.at[d], ret_recv.at[d], {"tp": z_at(d)})
    send(ret.at[pl.ds(1, 7), half], ret.at[pl.ds(1, 7), half], rsib_send, rsib_recv, {"seq": sib})

    for d in (1, 7, 2, 6, 3, 5, 4):
        arrived(done_in.at[d], d_send.at[d], d_recv.at[d], {"tp": z_at(d)})
        delta = delta + done_in[d].astype(F32)
    patch_out = (patch[0, 0].astype(F32) + delta).astype(BF16)
    arrived(ret.at[pl.ds(1, 7), other], rsib_send, rsib_recv, {"seq": sib})
    for d in (4, 3, 5, 2, 6, 1, 7):
        back_out[d] = dot(patch_out, ret[d]).astype(BF16)
        send(back_out.at[d], back_in.at[d], b_send.at[d], b_recv.at[d], {"tp": z_at(-d)})
    returned = dot(patch_out, ret[0])
    for d in (1, 7, 2, 6, 3, 5, 4):
        arrived(back_in.at[d], b_send.at[d], b_recv.at[d], {"tp": z_at(d)})
        returned = returned + back_in[d].astype(F32)
    returned = returned.astype(BF16)

    spread = lax.dot_general(
        onehot.astype(BF16), returned, (((0,), (0,)), ((), ())), preferred_element_type=F32
    )
    mixed = states.astype(F32) + spread
    ones = jnp.ones((8, 128), F32)
    sq_out[...] = lax.dot_general(
        ones, mixed * mixed, (((1,), (1,)), ((), ())),
        precision=lax.Precision.HIGHEST, preferred_element_type=F32,
    )
    for d in (4, 3, 5, 2, 6, 1, 7):
        send(sq_out, sq_in.at[d], q_send.at[d], q_recv.at[d], {"tp": z_at(d)})
    total = sq_out[...]
    for d in (1, 7, 2, 6, 3, 5, 4):
        arrived(sq_in.at[d], q_send.at[d], q_recv.at[d], {"tp": z_at(d)})
        total = total + sq_in[d]
    spread_sum = lax.dot_general(
        total, ones * 0.125, (((0,), (0,)), ((), ())),
        precision=lax.Precision.HIGHEST, preferred_element_type=F32,
    )
    out_ref[...] = (mixed * lax.rsqrt(spread_sum * (1.0 / DL) + EPS)).astype(BF16)
    for copy in started:
        copy.wait_send()


def on_device(
    byte_states, patch_map, lift_weight, gate_weight, up_weight, down_weight, return_weight
):
    vmem = pl.BlockSpec(memory_space=pltpu.VMEM)
    hbm = pl.BlockSpec(memory_space=pl.ANY)
    dma = pltpu.SemaphoreType.DMA
    out = pl.pallas_call(
        kernel,
        out_shape=jax.ShapeDtypeStruct((256, 128), BF16),
        in_specs=[vmem, vmem, hbm, hbm, hbm, hbm, hbm],
        out_specs=vmem,
        scratch_shapes=[
            pltpu.VMEM((128, 4096), BF16),
            pltpu.VMEM((16, 3, 256, 256), BF16),
            pltpu.VMEM((8, 64, 512), BF16),
            pltpu.VMEM((8, 64, 512), BF16),
            pltpu.VMEM((8, 4, 64, 512), BF16),
            pltpu.VMEM((2, 256, 256), F32),
            pltpu.VMEM((8, 4, 64, 512), BF16),
            pltpu.VMEM((8, 2, 64, 512), BF16),
            pltpu.VMEM((8, 64, 512), BF16),
            pltpu.VMEM((8, 64, 512), BF16),
            pltpu.VMEM((8, 64, 512), BF16),
            pltpu.VMEM((8, 64, 512), BF16),
            pltpu.VMEM((8, 512, 128), BF16),
            pltpu.VMEM((8, 64, 128), BF16),
            pltpu.VMEM((8, 64, 128), BF16),
            pltpu.VMEM((8, 256), F32),
            pltpu.VMEM((8, 8, 256), F32),
            dma((5,)),
            dma((2, 4, 2)), dma((2, 4, 2)),
            dma((8, 2)), dma((8, 2)),
            dma((8,)), dma((8,)),
            dma((2, 4)), dma((2, 4)),
            dma((8, 3)), dma((8, 3)),
            dma((8,)), dma((8,)),
            dma, dma,
            dma((8,)), dma((8,)),
            dma((8,)), dma((8,)),
            dma((8,)), dma((8,)),
            dma((8,)), dma((8,)),
            dma((8,)), dma((8,)),
        ],
        compiler_params=pltpu.CompilerParams(
            collective_id=0, has_side_effects=True, vmem_limit_bytes=48 * 1024 * 1024
        ),
    )(byte_states[0], patch_map, lift_weight, gate_weight, up_weight, down_weight, return_weight)
    return out[None]


def solution(mesh):
    placed = (
        P("grp", "seq", "tp"),
        P("grp", "seq"),
        P("tp", None),
        P("seq", ("grp", "tp")),
        P("seq", ("grp", "tp")),
        P(("grp", "tp"), "seq"),
        P(None, "tp"),
    )
    return jax.shard_map(
        on_device, mesh=mesh, in_specs=placed, out_specs=P("grp", "seq", "tp"), check_vma=False
    )
```

time: 543 us -> 101 us (0.19)
  the two profiles are of different devices: /device:TPU:8 before, /device:TPU:24 now
where the time goes in v1:
time: 101 us
  Pallas kernels  93.6 us (93%)
  local copies, waits for them, and re-layouts  7.31 us (7%)
    pallas_call x1, Pallas kernels, on_device(): pl.pallas_call(kernel, out_shape=jax.ShapeDtypeStruct((256, 128), BF16),...  93.6 us
    unnamed x15, local copies, waits for them, and re-layouts  7.31 us

profile of v1, /device:TPU:24, one launch (start us, length us, event | category | flops | bytes accessed | tf_op | source)
XLA Modules:
  0.0 100.9 jit_solution(4987627458435221129)
XLA Ops:
  0.0 0.0 copy-start.6
  0.0 0.7 copy-done.6
  0.7 0.0 copy-start
  0.7 1.2 %copy-done = bf16[128,4096]{1,0:T(8,128)(2,1)S(1)} copy-done((bf16[128,4096]{1,0:T(8,128)(2,1)S(1)}, bf16[128,4096]{1,0:T(8,128)(2,1)}, u32[]{:S(2)}) %copy-start) | copy-done | bytes 1048600
  1.9 0.0 copy-start.1
  1.9 1.2 %copy-done.1 = bf16[4096,128]{1,0:T(8,128)(2,1)S(1)} copy-done((bf16[4096,128]{1,0:T(8,128)(2,1)S(1)}, bf16[4096,128]{1,0:T(8,128)(2,1)}, u32[]{:S(2)}) %copy-start.1) | copy-done | bytes 1048600
  3.1 0.0 copy-start.2
  3.1 0.9 copy-done.2
  4.0 0.0 copy-start.3
  4.0 0.9 copy-done.3
  4.9 0.0 copy-start.4
  4.9 0.9 copy-done.4
  5.8 0.0 copy-start.5
  5.8 0.8 copy-done.5
  6.7 93.6 %shard_map.73 = bf16[256,128]{1,0:T(8,128)(2,1)S(1)} custom-call(bf16[256,128]{1,0:T(8,128)(2,1)S(1)} %bitcast.3, s32[1,256]{1,0:T(1,128)S(1)} %copy-done.6, bf16[128,4096]{1,0:T(8,128)(2,1)S(1)} %copy-done, bf16[256,256]{1,0:T(8,128)(2,1)S(1)} %copy-done.2, bf16[256,256]{1,0:T(8,128)(2,1)S(1)} %copy-done.3, bf16[256,256]{1,0:T(8,128)(2,1)S(1)} %copy-done.4, ...), custom_call_target="tpu_custom_call" | custom-call | tf_op jit(solution)/shard_map/pallas_call | solution.py:336
  100.3 0.6 copy.9
Async XLA Ops:
  0.0 0.7 copy-start.6
  0.7 1.2 %copy-start = (bf16[128,4096]{1,0:T(8,128)(2,1)S(1)}, bf16[128,4096]{1,0:T(8,128)(2,1)}, u32[]{:S(2)}) copy-start(bf16[128,4096]{1,0:T(8,128)(2,1)} %lift_hbm.1) | copy-start | bytes 3145732
  1.9 1.2 %copy-start.1 = (bf16[4096,128]{1,0:T(8,128)(2,1)S(1)}, bf16[4096,128]{1,0:T(8,128)(2,1)}, u32[]{:S(2)}) copy-start(bf16[4096,128]{1,0:T(8,128)(2,1)} %ret_hbm.1) | copy-start | bytes 3145732
  3.1 0.9 copy-start.2
  4.0 0.9 copy-start.3
  4.9 0.9 copy-start.4
  5.8 0.8 copy-start.5

commit v2 on v1

v2 whole, which is shorter than its diff:
```python
import jax
import jax.numpy as jnp
from jax import lax
from jax.experimental import pallas as pl
from jax.experimental.pallas import tpu as pltpu
from jax.sharding import PartitionSpec as P

DL = 1024
NMAX = 64
EPS = 1e-05
MESH = pl.DeviceIdType.MESH
F32 = jnp.float32
BF16 = jnp.bfloat16
IN_ORDER = (0, 1, 7, 2, 6, 3, 5, 4)


def dot(a, b):
    return jnp.dot(a, b, preferred_element_type=F32)


def kernel(
    states_ref, map_ref, lift_hbm, gate_hbm, up_hbm, down_hbm, ret_hbm, out_ref,
    lift, weights, lift_out, lift_in, patch, acc, down, ret, ret_rows, dr_own, dr_sib,
    dr_half, dr_in, dr, part, half_in, pair_out, pair_in, back_out, back_in, sq_out, sq_in,
    load_sem,
    y_sends, y_recvs,
    sib_sends, sib_recvs,
    lift_sends, lift_recvs,
    zg_sends, zg_recvs,
    xg_sends, xg_recvs,
    rz_sends, rz_recvs,
    rx_sends, rx_recvs,
    ds_sends, ds_recvs,
    dy_sends, dy_recvs,
    dg_sends, dg_recvs,
    dh_sends, dh_recvs,
    h_sends, h_recvs,
    p_sends, p_recvs,
    b_sends, b_recvs,
    q_sends, q_recvs,
):
    x = lax.axis_index("grp")
    s = lax.axis_index("seq")
    z = lax.axis_index("tp")
    y = s // 2
    c = s % 2
    xa = x + 1 - 2 * (x % 2)
    xb = 3 - x
    sib = 2 * y + 1 - c
    started = []
    y_sems = (y_sends, y_recvs)
    sib_sems = (sib_sends, sib_recvs)
    lift_sems = (lift_sends, lift_recvs)
    zg_sems = (zg_sends, zg_recvs)
    xg_sems = (xg_sends, xg_recvs)
    rz_sems = (rz_sends, rz_recvs)
    rx_sems = (rx_sends, rx_recvs)
    ds_sems = (ds_sends, ds_recvs)
    dy_sems = (dy_sends, dy_recvs)
    dg_sems = (dg_sends, dg_recvs)
    dh_sems = (dh_sends, dh_recvs)
    h_sems = (h_sends, h_recvs)
    p_sems = (p_sends, p_recvs)
    b_sems = (b_sends, b_recvs)
    q_sems = (q_sends, q_recvs)

    def z_at(d):
        return (z + d + 8) % 8

    def slot(q):
        return 2 * ((y + q + 8) % 8) + c

    def remote(src, dst, sems, index, device):
        return pltpu.make_async_remote_copy(
            src_ref=src, dst_ref=dst, send_sem=sems[0].at[index], recv_sem=sems[1].at[index],
            device_id=device, device_id_type=MESH,
        )

    def send(src, dst, sems, index, device):
        copy = remote(src, dst, sems, index, device)
        copy.start()
        started.append(copy)

    def arrived(ref, sems, index, device):
        remote(ref, ref, sems, index, device).wait_recv()

    loads = [
        pltpu.make_async_copy(lift_hbm, lift, load_sem.at[0]),
        pltpu.make_async_copy(gate_hbm, weights.at[s, 0], load_sem.at[1]),
        pltpu.make_async_copy(up_hbm, weights.at[s, 1], load_sem.at[2]),
        pltpu.make_async_copy(down_hbm, down, load_sem.at[3]),
        pltpu.make_async_copy(ret_hbm, ret, load_sem.at[4]),
    ]
    for load in loads:
        load.start()
    barrier = pltpu.get_barrier_semaphore()
    partners = [{"seq": slot(d)} for d in range(1, 8)] + [{"seq": sib}]
    partners += [{"grp": xa}, {"grp": xb}, {"grp": (x + 2) % 4}]
    partners += [{"tp": z_at(d)} for d in range(1, 8)]
    for partner in partners:
        pl.semaphore_signal(barrier, inc=1, device_id=partner, device_id_type=MESH)

    map_row = map_ref[...]
    onehot = (lax.broadcasted_iota(jnp.int32, (NMAX, 256), 0) == map_row).astype(F32)
    counts = jnp.sum(onehot, axis=1, keepdims=True)
    states = states_ref[...]
    sums = dot(onehot.astype(BF16), states)
    pooled = (sums / jnp.maximum(counts, 1.0)).astype(BF16)
    loads[0].wait()
    for k in range(8):
        lift_out[k] = dot(pooled, lift[:, 512 * k : 512 * (k + 1)]).astype(BF16)
    for load in loads[1:]:
        load.wait()
    pl.semaphore_wait(barrier, len(partners))

    def y_ref(q, way, hop):
        rows = pl.ds(0, 256) if hop < 3 else pl.ds(128 * way, 128)
        return weights.at[slot(q), :, rows]

    def y_go(way, hop):
        ref = y_ref(-hop if way == 0 else hop, way, hop)
        send(ref, ref, y_sems, (way, hop), {"seq": slot(1 if way == 0 else -1)})

    def sib_go(q):
        ref = weights.at[slot(q)]
        send(ref, ref, sib_sems, (q % 8,), {"seq": sib})

    def y_step(hop):
        for way in (0, 1):
            q = -(hop + 1) if way == 0 else hop + 1
            arrived(y_ref(q, way, hop), y_sems, (way, hop), {"seq": slot(1)})
            if hop < 3:
                y_go(way, hop + 1)
                sib_go(q)
        if hop == 3:
            sib_go(4)

    def sib_wait():
        for k in range(8):
            arrived(weights.at[2 * ((y + k) % 8) + 1 - c], sib_sems, (k,), {"seq": sib})

    quarter = pl.ds(64 * x, 64)
    own_rows = pl.ds(256 * s + 64 * x, 64)
    for d in (4, 3, 5, 2, 6, 1, 7):
        send(ret.at[own_rows], ret_rows.at[d, quarter], rz_sems, (d,), {"tp": z_at(d)})
    y_go(0, 0)
    y_go(1, 0)
    sib_go(0)
    for d in (4, 3, 5, 2, 6, 1, 7):
        send(lift_out.at[z_at(d)], lift_in.at[d], lift_sems, (d,), {"tp": z_at(d)})
    ret_rows[0, quarter] = ret[own_rows]
    for d in (1, 7, 2, 6, 3, 5, 4):
        arrived(ret_rows.at[d, quarter], rz_sems, (d,), {"tp": z_at(d)})
    for j in (2, 1, 3):
        ref = ret_rows.at[:, quarter]
        send(ref, ref, rx_sems, (j,), {"grp": (x + j) % 4})

    y_step(0)

    for j in (1, 3, 2):
        arrived(ret_rows.at[:, quarter], rx_sems, (j,), {"grp": xa})
    down_own = down[...]
    for d in range(8):
        dr_own[d] = dot(down_own, ret_rows[d]).astype(BF16)
    mine = pl.ds(4 * c, 4)
    send(dr_own.at[pl.ds(4 - 4 * c, 4)], dr_sib, ds_sems, (0,), {"seq": sib})
    arrived(dr_sib, ds_sems, (0,), {"seq": sib})
    dr_half[...] = (dr_own[mine].astype(F32) + dr_sib[...].astype(F32)).astype(BF16)

    def units(q):
        return pl.ds(32 * ((y + q + 8) % 8), 32)

    for q in (4, 3, 5, 2, 6, 1, 7):
        send(dr_half.at[:, units(q)], dr_in.at[q], dy_sems, (q,), {"seq": slot(q)})

    block = lift_out[z].astype(F32)
    for d in (1, 7, 2, 6, 3, 5, 4):
        arrived(lift_in.at[d], lift_sems, (d,), {"tp": z_at(d)})
        block = block + lift_in[d].astype(F32)
    patch[0, 0] = block.astype(BF16)

    def zg_ref(e, way, hop):
        rows = pl.ds(0, 64) if hop < 3 else pl.ds(32 * way, 32)
        return patch.at[e, 0, rows]

    def zg_go(way, hop):
        e = hop if way == 0 else (8 - hop) % 8
        e2 = hop + 1 if way == 0 else 7 - hop
        send(zg_ref(e, way, hop), zg_ref(e2, way, hop), zg_sems, (way, hop,), {"tp": z_at(1 if way == 0 else -1)})

    def zg_wait(way, hop):
        e = hop + 1 if way == 0 else 7 - hop
        arrived(zg_ref(e, way, hop), zg_sems, (way, hop,),
                {"tp": z_at(1)})

    def first_second(i):
        return ((xa, 1), (xb, 3)) if i % 2 == 0 else ((xb, 3), (xa, 1))

    def xg_one(i):
        e = IN_ORDER[i]
        (n1, j1), _ = first_second(i)
        send(patch.at[e, 0], patch.at[e, j1], xg_sems, (e, 0,), {"grp": n1})

    def xg_two(i):
        e = IN_ORDER[i]
        (n1, j1), (n2, j2) = first_second(i)
        send(patch.at[e, 0], patch.at[e, j2], xg_sems, (e, 1,), {"grp": n2})
        arrived(patch.at[e, j1], xg_sems, (e, 0,), {"grp": n1})
        send(patch.at[e, j1], patch.at[e, 2], xg_sems, (e, 2,), {"grp": n2})

    def xg_wait(i):
        e = IN_ORDER[i]
        _, (n2, j2) = first_second(i)
        arrived(patch.at[e, j2], xg_sems, (e, 1,), {"grp": n2})
        arrived(patch.at[e, 2], xg_sems, (e, 2,), {"grp": n2})

    zg_go(0, 0)
    zg_go(1, 0)
    xg_one(0)
    y_step(1)
    zg_wait(0, 0)
    zg_go(0, 1)
    xg_one(1)
    zg_wait(1, 0)
    zg_go(1, 1)
    xg_one(2)
    xg_two(0)

    total = dr_half[:, units(0)].astype(F32)
    for q in (1, 7, 2, 6, 3, 5, 4):
        arrived(dr_in.at[q], dy_sems, (q,), {"seq": slot(q)})
        total = total + dr_in[q].astype(F32)
    dr[mine, units(0)] = total.astype(BF16)
    for q in (4, 3, 5, 2, 6, 1, 7):
        ref = dr.at[mine, units(0)]
        send(ref, ref, dg_sems, (q,), {"seq": slot(q)})

    zg_wait(0, 1)
    zg_go(0, 2)
    xg_one(3)
    zg_wait(1, 1)
    zg_go(1, 2)
    xg_one(4)
    xg_two(1)
    xg_two(2)
    y_step(2)
    zg_wait(0, 2)
    zg_go(0, 3)
    xg_one(5)
    zg_wait(1, 2)
    zg_go(1, 3)
    xg_one(6)
    xg_two(3)
    xg_two(4)
    zg_wait(0, 3)
    zg_wait(1, 3)
    xg_one(7)
    xg_two(5)
    xg_two(6)
    y_step(3)
    for q in (1, 7, 2, 6, 3, 5, 4):
        arrived(dr.at[mine, units(-q)], dg_sems, (q,), {"seq": slot(q)})
    send(dr.at[mine], dr.at[mine], dh_sems, (0,), {"seq": sib})
    xg_two(7)
    sib_wait()

    squares = jnp.zeros((256, 1), F32)
    returned = jnp.zeros((64, 128), F32)
    for i in range(8):
        e = IN_ORDER[i]
        xg_wait(i)
        kb = z_at(-e)
        rows = patch[e].reshape(256, 512)
        returned = returned + dot(patch[e, 0], ret[pl.ds(512 * kb, 512)])
        wide = rows.astype(F32)
        squares = squares + jnp.sum(wide * wide, axis=1, keepdims=True)
        for a in (0, 1):
            w = weights[pl.ds(2 * kb, 2), a].reshape(512, 256)
            if i == 0:
                acc[a] = dot(rows, w)
            else:
                acc[a] += dot(rows, w)
    scale = lax.rsqrt(squares * (1.0 / 4096) + EPS)
    gate = acc[0] * scale
    up = acc[1] * scale
    hidden = (gate / (1.0 + jnp.exp(-gate)) * up).astype(BF16)

    arrived(dr.at[pl.ds(4 - 4 * c, 4)], dh_sems, (0,), {"seq": sib})

    def down_one(i):
        for n in (0, 1):
            part[i, n] = dot(hidden, dr[2 * i + n]).astype(BF16).reshape(4, 64, 128)
        (n1, j1), _ = first_second(i)
        src = part.at[i, :, pl.ds(1 if j1 == 1 else 2, 2)]
        send(src, half_in.at[i], h_sems, (i,), {"grp": n1})

    def down_two(i):
        (n1, j1), (n2, j2) = first_second(i)
        arrived(half_in.at[i], h_sems, (i,), {"grp": n1})
        row = 1 if j1 == 1 else 0
        pair_out[i] = (part[i, :, j2].astype(F32) + half_in[i, :, row].astype(F32)).astype(BF16)
        send(pair_out.at[i], pair_in.at[i], p_sems, (i,), {"grp": n2})

    def down_three(i):
        (n1, j1), (n2, j2) = first_second(i)
        arrived(pair_in.at[i], p_sems, (i,), {"grp": n2})
        row = 0 if j1 == 1 else 1
        for n in (0, 1):
            total = part[i, n, 0].astype(F32) + half_in[i, n, row].astype(F32)
            total = total + pair_in[i, n].astype(F32)
            d = 2 * i + n
            if d == 0:
                own_total.append(total)
            else:
                back_out[d] = total.astype(BF16)
                send(back_out.at[d], back_in.at[d], b_sems, (d,), {"tp": z_at(-d)})

    own_total = []
    order = (2, 1, 3, 0)
    for i in order:
        down_one(i)
    for n in range(5):
        if n < 4:
            down_two(order[n])
        if n > 0:
            down_three(order[n - 1])

    returned = returned + own_total[0]
    for d in (1, 7, 2, 6, 3, 5, 4):
        arrived(back_in.at[d], b_sems, (d,), {"tp": z_at(d)})
        returned = returned + back_in[d].astype(F32)
    returned = returned.astype(BF16)

    spread = lax.dot_general(
        onehot.astype(BF16), returned, (((0,), (0,)), ((), ())), preferred_element_type=F32
    )
    mixed = states.astype(F32) + spread
    ones = jnp.ones((8, 128), F32)
    sq_out[...] = lax.dot_general(
        ones, mixed * mixed, (((1,), (1,)), ((), ())),
        precision=lax.Precision.HIGHEST, preferred_element_type=F32,
    )
    for d in (4, 3, 5, 2, 6, 1, 7):
        send(sq_out, sq_in.at[d], q_sems, (d,), {"tp": z_at(d)})
    total = sq_out[...]
    for d in (1, 7, 2, 6, 3, 5, 4):
        arrived(sq_in.at[d], q_sems, (d,), {"tp": z_at(d)})
        total = total + sq_in[d]
    spread_sum = lax.dot_general(
        total, ones * 0.125, (((0,), (0,)), ((), ())),
        precision=lax.Precision.HIGHEST, preferred_element_type=F32,
    )
    out_ref[...] = (mixed * lax.rsqrt(spread_sum * (1.0 / DL) + EPS)).astype(BF16)
    for copy in started:
        copy.wait_send()


def on_device(
    byte_states, patch_map, lift_weight, gate_weight, up_weight, down_weight, return_weight
):
    vmem = pl.BlockSpec(memory_space=pltpu.VMEM)
    hbm = pl.BlockSpec(memory_space=pl.ANY)
    dma = pltpu.SemaphoreType.DMA
    out = pl.pallas_call(
        kernel,
        out_shape=jax.ShapeDtypeStruct((256, 128), BF16),
        in_specs=[vmem, vmem, hbm, hbm, hbm, hbm, hbm],
        out_specs=vmem,
        scratch_shapes=[
            pltpu.VMEM((128, 4096), BF16),
            pltpu.VMEM((16, 2, 256, 256), BF16),
            pltpu.VMEM((8, 64, 512), BF16),
            pltpu.VMEM((8, 64, 512), BF16),
            pltpu.VMEM((8, 4, 64, 512), BF16),
            pltpu.VMEM((2, 256, 256), F32),
            pltpu.VMEM((256, 256), BF16),
            pltpu.VMEM((4096, 128), BF16),
            pltpu.VMEM((8, 256, 128), BF16),
            pltpu.VMEM((8, 256, 128), BF16),
            pltpu.VMEM((4, 256, 128), BF16),
            pltpu.VMEM((4, 256, 128), BF16),
            pltpu.VMEM((8, 4, 32, 128), BF16),
            pltpu.VMEM((8, 256, 128), BF16),
            pltpu.VMEM((4, 2, 4, 64, 128), BF16),
            pltpu.VMEM((4, 2, 2, 64, 128), BF16),
            pltpu.VMEM((4, 2, 64, 128), BF16),
            pltpu.VMEM((4, 2, 64, 128), BF16),
            pltpu.VMEM((8, 64, 128), BF16),
            pltpu.VMEM((8, 64, 128), BF16),
            pltpu.VMEM((8, 256), F32),
            pltpu.VMEM((8, 8, 256), F32),
            dma((5,)),
            dma((2, 4)), dma((2, 4)),
            dma((8,)), dma((8,)),
            dma((8,)), dma((8,)),
            dma((2, 4)), dma((2, 4)),
            dma((8, 3)), dma((8, 3)),
            dma((8,)), dma((8,)),
            dma((4,)), dma((4,)),
            dma((1,)), dma((1,)),
            dma((8,)), dma((8,)),
            dma((8,)), dma((8,)),
            dma((1,)), dma((1,)),
            dma((4,)), dma((4,)),
            dma((4,)), dma((4,)),
            dma((8,)), dma((8,)),
            dma((8,)), dma((8,)),
        ],
        compiler_params=pltpu.CompilerParams(
            collective_id=0, has_side_effects=True, vmem_limit_bytes=64 * 1024 * 1024
        ),
    )(byte_states[0], patch_map, lift_weight, gate_weight, up_weight, down_weight, return_weight)
    return out[None]


def solution(mesh):
    placed = (
        P("grp", "seq", "tp"),
        P("grp", "seq"),
        P("tp", None),
        P("seq", ("grp", "tp")),
        P("seq", ("grp", "tp")),
        P(("grp", "tp"), "seq"),
        P(None, "tp"),
    )
    return jax.shard_map(
        on_device, mesh=mesh, in_specs=placed, out_specs=P("grp", "seq", "tp"), check_vma=False
    )
```

time: 101 us -> 81.4 us (0.81)
  the two profiles are of different devices: /device:TPU:24 before, /device:TPU:2 now
where the time goes in v2:
time: 81.4 us; the launch traced here: 81.2 us
  Pallas kernels  79.7 us (98%)
  local copies, waits for them, and re-layouts  1.47 us (2%)
    pallas_call x1, Pallas kernels, on_device(): pl.pallas_call(kernel, out_shape=jax.ShapeDtypeStruct((256, 128), BF16),...  79.7 us

profile of v2, /device:TPU:2, one launch (start us, length us, event | category | flops | bytes accessed | tf_op | source)
XLA Modules:
  0.0 81.2 jit_solution(1925637886637105063)
XLA Ops:
  0.0 79.7 %shard_map.73 = bf16[256,128]{1,0:T(8,128)(2,1)} custom-call(bf16[256,128]{1,0:T(8,128)(2,1)} %bitcast.3, s32[1,256]{1,0:T(1,128)} %map_ref.1, bf16[128,4096]{1,0:T(8,128)(2,1)} %lift_hbm.1, bf16[256,256]{1,0:T(8,128)(2,1)} %gate_hbm.1, bf16[256,256]{1,0:T(8,128)(2,1)} %up_hbm.1, bf16[256,256]{1,0:T(8,128)(2,1)} %down_hbm.1, bf16[4096,128]{1,0:T(8,128)(2,1)} %ret_hbm.1), custom_call_target="tpu_custom_call" | custom-call | tf_op jit(solution)/shard_map/pallas_call | solution.py:364
  79.7 1.5 %copy.9 = bf16[1,256,128]{2,1,0:T(8,128)(2,1)} copy(bf16[1,256,128]{2,1,0:T(8,128)(2,1)} %bitcast.2) | data formatting | bytes 131072

commit v3 on v2

v3 whole, which is shorter than its diff:
```python
import jax
import jax.numpy as jnp
from jax import lax
from jax.experimental import pallas as pl
from jax.experimental.pallas import tpu as pltpu
from jax.sharding import PartitionSpec as P

DL = 1024
NMAX = 64
EPS = 1e-05
MESH = pl.DeviceIdType.MESH
F32 = jnp.float32
BF16 = jnp.bfloat16
IN_ORDER = (0, 1, 7, 2, 6, 3, 5, 4)


def dot(a, b):
    return jnp.dot(a, b, preferred_element_type=F32)


def kernel(
    states_hbm, map_hbm, lift_hbm, gate_hbm, up_hbm, down_hbm, ret_hbm, out_ref,
    slots, states_vmem, onehot_t, lift, weights, lift_out, lift_sum, lift_in, patch, acc,
    down, ret, ret_rows, dr_half, dr_in, dr, part, half_in, pair_out, pair_in, back_out, back_in, sq_out, sq_in,
    load_sem,
    y_sends, y_recvs,
    sib_sends, sib_recvs,
    lift_sends, lift_recvs,
    za_sends, za_recvs,
    xg_sends, xg_recvs,
    rz_sends, rz_recvs,
    rx_sends, rx_recvs,
    dn_sends, dn_recvs,
    dy_sends, dy_recvs,
    dg_sends, dg_recvs,
    dh_sends, dh_recvs,
    h_sends, h_recvs,
    p_sends, p_recvs,
    b_sends, b_recvs,
    q_sends, q_recvs,
):
    x = lax.axis_index("grp")
    s = lax.axis_index("seq")
    z = lax.axis_index("tp")
    y = s // 2
    c = s % 2
    xa = x + 1 - 2 * (x % 2)
    xb = 3 - x
    sib = 2 * y + 1 - c
    started = []
    y_sems = (y_sends, y_recvs)
    sib_sems = (sib_sends, sib_recvs)
    lift_sems = (lift_sends, lift_recvs)
    za_sems = (za_sends, za_recvs)
    xg_sems = (xg_sends, xg_recvs)
    rz_sems = (rz_sends, rz_recvs)
    rx_sems = (rx_sends, rx_recvs)
    dn_sems = (dn_sends, dn_recvs)
    dy_sems = (dy_sends, dy_recvs)
    dg_sems = (dg_sends, dg_recvs)
    dh_sems = (dh_sends, dh_recvs)
    h_sems = (h_sends, h_recvs)
    p_sems = (p_sends, p_recvs)
    b_sems = (b_sends, b_recvs)
    q_sems = (q_sends, q_recvs)

    def z_at(d):
        return (z + d + 8) % 8

    def slot(q):
        return 2 * ((y + q + 8) % 8) + c

    def remote(src, dst, sems, index, device):
        return pltpu.make_async_remote_copy(
            src_ref=src, dst_ref=dst, send_sem=sems[0].at[index], recv_sem=sems[1].at[index],
            device_id=device, device_id_type=MESH,
        )

    def send(src, dst, sems, index, device):
        copy = remote(src, dst, sems, index, device)
        copy.start()
        started.append(copy)

    def arrived(ref, sems, index, device):
        remote(ref, ref, sems, index, device).wait_recv()

    loads = [
        pltpu.make_async_copy(map_hbm, slots, load_sem.at[0]),
        pltpu.make_async_copy(states_hbm.at[0], states_vmem, load_sem.at[1]),
        pltpu.make_async_copy(lift_hbm, lift, load_sem.at[2]),
        pltpu.make_async_copy(gate_hbm, weights.at[s, 0], load_sem.at[3]),
        pltpu.make_async_copy(up_hbm, weights.at[s, 1], load_sem.at[4]),
        pltpu.make_async_copy(down_hbm, down.at[c], load_sem.at[5]),
        pltpu.make_async_copy(ret_hbm, ret, load_sem.at[6]),
    ]
    for load in loads:
        load.start()
    barrier = pltpu.get_barrier_semaphore()
    partners = [{"seq": slot(d)} for d in range(1, 8)] + [{"seq": sib}]
    partners += [{"grp": xa}, {"grp": xb}, {"grp": (x + 2) % 4}]
    partners += [{"tp": z_at(d)} for d in range(1, 8)]
    for partner in partners:
        pl.semaphore_signal(barrier, inc=1, device_id=partner, device_id_type=MESH)

    pl.semaphore_wait(barrier, len(partners))

    def y_ref(q, way, hop):
        rows = pl.ds(0, 256) if hop < 3 else pl.ds(128 * way, 128)
        return weights.at[slot(q), :, rows]

    def y_go(way, hop):
        device = {"seq": slot(1 if way == 0 else -1)}
        if hop == 0:
            send(gate_hbm, weights.at[s, 0], y_sems, (way, 0), device)
            send(up_hbm, weights.at[s, 1], y_sems, (way, 4), device)
        else:
            ref = y_ref(-hop if way == 0 else hop, way, hop)
            send(ref, ref, y_sems, (way, hop), device)

    def sib_go(q):
        ref = weights.at[slot(q)]
        send(ref, ref, sib_sems, (q % 8,), {"seq": sib})

    def y_step(hop):
        for way in (0, 1):
            q = -(hop + 1) if way == 0 else hop + 1
            if hop == 0:
                arrived(weights.at[slot(q), 0], y_sems, (way, 0), {"seq": slot(1)})
                arrived(weights.at[slot(q), 1], y_sems, (way, 4), {"seq": slot(1)})
            else:
                arrived(y_ref(q, way, hop), y_sems, (way, hop), {"seq": slot(1)})
            if hop < 3:
                y_go(way, hop + 1)
                sib_go(q)
        if hop == 3:
            sib_go(4)

    def sib_wait():
        for k in range(8):
            arrived(weights.at[2 * ((y + k) % 8) + 1 - c], sib_sems, (k,), {"seq": sib})

    for k in (1, 2, 3):
        send(ret_hbm.at[y, :, x], ret_rows.at[k, :, x], rz_sems, (k,), {"tp": z_at(4 * c + k)})

    def across():
        return remote(ret_hbm.at[y, :, x], ret_rows.at[0, :, x], rz_sems, (0,), {"tp": z_at(4)})

    @pl.when(c == 1)
    def _():
        across().start()

    send(down_hbm, down.at[c], dn_sems, (0,), {"seq": sib})
    y_go(0, 0)
    y_go(1, 0)

    for load in loads[:2]:
        load.wait()
    onehot = (lax.broadcasted_iota(jnp.int32, (NMAX, 256), 0) == slots[...]).astype(F32)
    counts = jnp.sum(onehot, axis=1, keepdims=True)
    states = states_vmem[...]
    sums = dot(onehot.astype(BF16), states)
    pooled = (sums / jnp.maximum(counts, 1.0)).astype(BF16)
    loads[2].wait()

    def lift_go(way, hop):
        device = {"tp": z_at(1 if way == 0 else -1)}
        if hop == 0:
            rows = pl.ds(32 * way, 32)
            send(lift_out.at[4, rows], lift_in.at[way, 0, rows], lift_sems, (way, 0), device)
        else:
            send(lift_sum.at[way, hop], lift_in.at[way, hop], lift_sems, (way, hop), device)

    def lift_arrived(way, hop):
        rows = pl.ds(32 * way, 32) if hop == 0 else pl.ds(0, 64)
        arrived(lift_in.at[way, hop, rows], lift_sems, (way, hop), {"tp": z_at(1)})

    def lift_step(hop):
        for way in (0, 1):
            lift_arrived(way, hop)
            d = 3 - hop if way == 0 else 5 + hop
            if hop == 0:
                rows = pl.ds(32 * way, 32)
                rest = pl.ds(32 * (1 - way), 32)
                lift_sum[way, 1, rest] = lift_out[d, rest]
                lift_sum[way, 1, rows] = (
                    lift_out[d, rows].astype(F32) + lift_in[way, 0, rows].astype(F32)
                ).astype(BF16)
            else:
                lift_sum[way, hop + 1] = (
                    lift_out[d].astype(F32) + lift_in[way, hop].astype(F32)
                ).astype(BF16)
            lift_go(way, hop + 1)

    for d in (4, 3, 5, 2, 6, 1, 7, 0):
        columns = lift[:, pl.ds(pl.multiple_of(512 * z_at(d), 512), 512)]
        lift_out[d] = dot(pooled, columns).astype(BF16)
        if d == 4:
            lift_go(0, 0)
            lift_go(1, 0)
    onehot_t[...] = jnp.transpose(onehot).astype(BF16)
    for load in loads[3:]:
        load.wait()
    sib_go(0)

    @pl.when(c == 0)
    def _():
        ret_rows[0, :, x] = ret[y, :, x]

    def ret_x():
        for k in (1, 2, 3):
            arrived(ret_rows.at[k, :, x], rz_sems, (k,), {"tp": z_at(1)})

        @pl.when(c == 1)
        def _():
            across().wait_recv()

        for j in (2, 1, 3):
            ref = ret_rows.at[:, :, x]
            send(ref, ref, rx_sems, (j,), {"grp": (x + j) % 4})

    mine = pl.ds(4 * c, 4)

    def units(q):
        return pl.ds(32 * ((y + q + 8) % 8), 32)

    def dr_products():
        for j in (1, 3, 2):
            arrived(ret_rows.at[:, :, x], rx_sems, (j,), {"grp": xa})
        arrived(down.at[1 - c], dn_sems, (0,), {"seq": sib})
        for k in range(4):
            val = dot(down[0], ret_rows[k, 0].reshape(256, 128))
            val = val + dot(down[1], ret_rows[k, 1].reshape(256, 128))
            dr_half[k] = val.astype(BF16)
        for q in (4, 3, 5, 2, 6, 1, 7):
            send(dr_half.at[:, units(q)], dr_in.at[q], dy_sems, (q,), {"seq": slot(q)})

    def dr_total():
        total = dr_half[:, units(0)].astype(F32)
        for q in (1, 7, 2, 6, 3, 5, 4):
            arrived(dr_in.at[q], dy_sems, (q,), {"seq": slot(q)})
            total = total + dr_in[q].astype(F32)
        dr[mine, units(0)] = total.astype(BF16)
        for q in (4, 3, 5, 2, 6, 1, 7):
            ref = dr.at[mine, units(0)]
            send(ref, ref, dg_sems, (q,), {"seq": slot(q)})

    def dr_share():
        for q in (1, 7, 2, 6, 3, 5, 4):
            arrived(dr.at[mine, units(-q)], dg_sems, (q,), {"seq": slot(q)})
        send(dr.at[mine], dr.at[mine], dh_sems, (0,), {"seq": sib})

    def ring_places(way, hop):
        return (hop, hop + 1) if way == 0 else ((8 - hop) % 8, 7 - hop)

    def za_ref(e, way, hop):
        rows = pl.ds(0, 64) if hop < 3 else pl.ds(32 * way, 32)
        return patch.at[e, 0, rows]

    def za_go(way, hop):
        e, e2 = ring_places(way, hop)
        send(za_ref(e, way, hop), za_ref(e2, way, hop), za_sems, (way, hop),
             {"tp": z_at(1 if way == 0 else -1)})

    def first_second(i):
        return ((xa, 1), (xb, 3)) if i % 2 == 0 else ((xb, 3), (xa, 1))

    def xg_one(i):
        e = IN_ORDER[i]
        (n1, j1), _ = first_second(i)
        send(patch.at[e, 0], patch.at[e, j1], xg_sems, (e, 0), {"grp": n1})

    def xg_two(i):
        e = IN_ORDER[i]
        (n1, j1), (n2, j2) = first_second(i)
        send(patch.at[e, 0], patch.at[e, j2], xg_sems, (e, 1), {"grp": n2})
        arrived(patch.at[e, j1], xg_sems, (e, 0), {"grp": n1})
        send(patch.at[e, j1], patch.at[e, 2], xg_sems, (e, 2), {"grp": n2})

    def xg_wait(i):
        e = IN_ORDER[i]
        _, (n2, j2) = first_second(i)
        arrived(patch.at[e, j2], xg_sems, (e, 1), {"grp": n2})
        arrived(patch.at[e, 2], xg_sems, (e, 2), {"grp": n2})

    def za_step(hop):
        for way in (0, 1):
            e2 = ring_places(way, hop)[1]
            arrived(za_ref(e2, way, hop), za_sems, (way, hop), {"tp": z_at(1)})
            if hop < 3:
                za_go(way, hop + 1)
                xg_one(2 * hop + 1 + way)
        if hop == 3:
            xg_one(7)

    def patch_start():
        block = lift_out[0].astype(F32)
        for way in (0, 1):
            lift_arrived(way, 3)
            block = block + lift_in[way, 3].astype(F32)
        patch[0, 0] = block.astype(BF16)
        za_go(0, 0)
        za_go(1, 0)
        xg_one(0)

    lift_step(0)
    ret_x()
    lift_step(1)
    y_step(0)
    lift_step(2)
    dr_products()
    patch_start()
    y_step(1)
    za_step(0)
    xg_two(0)
    za_step(1)
    xg_two(1)
    xg_two(2)
    za_step(2)
    y_step(2)
    xg_two(3)
    xg_two(4)
    za_step(3)
    dr_total()
    xg_two(5)
    xg_two(6)
    y_step(3)
    xg_two(7)

    squares = jnp.zeros((256, 1), F32)
    returned = jnp.zeros((64, 128), F32)

    def multiply(i, squares, returned):
        xg_wait(i)
        e = IN_ORDER[i]
        kb = z_at(-e)
        rows = patch[e].reshape(256, 512)
        returned = returned + dot(patch[e, 0], ret[kb].reshape(512, 128))
        wide = rows.astype(F32)
        squares = squares + jnp.sum(wide * wide, axis=1, keepdims=True)
        for a in (0, 1):
            w = weights[pl.ds(2 * kb, 2), a].reshape(512, 256)
            if i == 0:
                acc[a] = dot(rows, w)
            else:
                acc[a] += dot(rows, w)
        return squares, returned

    sib_wait()
    for i in range(6):
        squares, returned = multiply(i, squares, returned)
    dr_share()
    for i in range(6, 8):
        squares, returned = multiply(i, squares, returned)

    scale = lax.rsqrt(squares * (1.0 / 4096) + EPS)
    gate = acc[0] * scale
    up = acc[1] * scale
    hidden = (gate / (1.0 + jnp.exp(-gate)) * up).astype(BF16)

    arrived(dr.at[pl.ds(4 - 4 * c, 4)], dh_sems, (0,), {"seq": sib})

    def down_one(i):
        for n in (0, 1):
            part[i, n] = dot(hidden, dr[2 * i + n]).astype(BF16).reshape(4, 64, 128)
        (n1, j1), _ = first_second(i)
        src = part.at[i, :, pl.ds(1 if j1 == 1 else 2, 2)]
        send(src, half_in.at[i], h_sems, (i,), {"grp": n1})

    def down_two(i):
        (n1, j1), (n2, j2) = first_second(i)
        arrived(half_in.at[i], h_sems, (i,), {"grp": n1})
        row = 1 if j1 == 1 else 0
        pair_out[i] = (part[i, :, j2].astype(F32) + half_in[i, :, row].astype(F32)).astype(BF16)
        send(pair_out.at[i], pair_in.at[i], p_sems, (i,), {"grp": n2})

    def down_three(i):
        (n1, j1), (n2, j2) = first_second(i)
        arrived(pair_in.at[i], p_sems, (i,), {"grp": n2})
        row = 0 if j1 == 1 else 1
        for n in (0, 1):
            total = part[i, n, 0].astype(F32) + half_in[i, n, row].astype(F32)
            total = total + pair_in[i, n].astype(F32)
            d = 2 * i + n
            if d == 0:
                own_total.append(total)
            else:
                back_out[d] = total.astype(BF16)
                send(back_out.at[d], back_in.at[d], b_sems, (d,), {"tp": z_at(-d)})

    own_total = []
    order = (2, 1, 3, 0)
    for i in order:
        down_one(i)
    for n in range(5):
        if n < 4:
            down_two(order[n])
        if n > 0:
            down_three(order[n - 1])

    returned = returned + own_total[0]
    for d in (1, 7, 2, 6, 3, 5, 4):
        arrived(back_in.at[d], b_sems, (d,), {"tp": z_at(d)})
        returned = returned + back_in[d].astype(F32)
    returned = returned.astype(BF16)

    mixed = states_vmem[...].astype(F32) + dot(onehot_t[...], returned)
    square = mixed * mixed
    upper = square.astype(BF16)
    lower = (square - upper.astype(F32)).astype(BF16)
    ones = jnp.ones((8, 128), BF16)
    dims = (((1,), (1,)), ((), ()))
    sq_out[...] = lax.dot_general(ones, upper, dims, preferred_element_type=F32) + (
        lax.dot_general(ones, lower, dims, preferred_element_type=F32)
    )
    for d in (4, 3, 5, 2, 6, 1, 7):
        send(sq_out, sq_in.at[d], q_sems, (d,), {"tp": z_at(d)})
    total = sq_out[...]
    for d in (1, 7, 2, 6, 3, 5, 4):
        arrived(sq_in.at[d], q_sems, (d,), {"tp": z_at(d)})
        total = total + sq_in[d]
    inverse = lax.rsqrt(total[0:1] * (1.0 / DL) + EPS)
    inverse = jnp.transpose(jnp.broadcast_to(inverse, (128, 256)))
    out_ref[...] = (mixed * inverse).astype(BF16)

    @pl.when(c == 1)
    def _():
        across().wait_send()

    for copy in started:
        copy.wait_send()


def on_device(
    byte_states, patch_map, lift_weight, gate_weight, up_weight, down_weight, return_weight
):
    vmem = pl.BlockSpec(memory_space=pltpu.VMEM)
    hbm = pl.BlockSpec(memory_space=pl.ANY)
    dma = pltpu.SemaphoreType.DMA
    out = pl.pallas_call(
        kernel,
        out_shape=jax.ShapeDtypeStruct((256, 128), BF16),
        in_specs=[hbm] * 7,
        out_specs=vmem,
        scratch_shapes=[
            pltpu.VMEM((1, 256), jnp.int32),
            pltpu.VMEM((256, 128), BF16),
            pltpu.VMEM((256, 64), BF16),
            pltpu.VMEM((128, 4096), BF16),
            pltpu.VMEM((16, 2, 256, 256), BF16),
            pltpu.VMEM((8, 64, 512), BF16),
            pltpu.VMEM((2, 4, 64, 512), BF16),
            pltpu.VMEM((2, 4, 64, 512), BF16),
            pltpu.VMEM((8, 4, 64, 512), BF16),
            pltpu.VMEM((2, 256, 256), F32),
            pltpu.VMEM((2, 256, 256), BF16),
            pltpu.VMEM((8, 2, 4, 64, 128), BF16),
            pltpu.VMEM((4, 2, 4, 64, 128), BF16),
            pltpu.VMEM((4, 256, 128), BF16),
            pltpu.VMEM((8, 4, 32, 128), BF16),
            pltpu.VMEM((8, 256, 128), BF16),
            pltpu.VMEM((4, 2, 4, 64, 128), BF16),
            pltpu.VMEM((4, 2, 2, 64, 128), BF16),
            pltpu.VMEM((4, 2, 64, 128), BF16),
            pltpu.VMEM((4, 2, 64, 128), BF16),
            pltpu.VMEM((8, 64, 128), BF16),
            pltpu.VMEM((8, 64, 128), BF16),
            pltpu.VMEM((8, 256), F32),
            pltpu.VMEM((8, 8, 256), F32),
            dma((7,)),
            dma((2, 5)), dma((2, 5)),
            dma((8,)), dma((8,)),
            dma((2, 4)), dma((2, 4)),
            dma((2, 4)), dma((2, 4)),
            dma((8, 3)), dma((8, 3)),
            dma((4,)), dma((4,)),
            dma((4,)), dma((4,)),
            dma((1,)), dma((1,)),
            dma((8,)), dma((8,)),
            dma((8,)), dma((8,)),
            dma((1,)), dma((1,)),
            dma((4,)), dma((4,)),
            dma((4,)), dma((4,)),
            dma((8,)), dma((8,)),
            dma((8,)), dma((8,)),
        ],
        compiler_params=pltpu.CompilerParams(
            collective_id=0, has_side_effects=True, vmem_limit_bytes=64 * 1024 * 1024
        ),
    )(
        byte_states, patch_map, lift_weight, gate_weight, up_weight, down_weight,
        return_weight.reshape(8, 2, 4, 64, 128),
    )
    return out[None]


def solution(mesh):
    placed = (
        P("grp", "seq", "tp"),
        P("grp", "seq"),
        P("tp", None),
        P("seq", ("grp", "tp")),
        P("seq", ("grp", "tp")),
        P(("grp", "tp"), "seq"),
        P(None, "tp"),
    )
    return jax.shard_map(
        on_device, mesh=mesh, in_specs=placed, out_specs=P("grp", "seq", "tp"), check_vma=False
    )
```

time: 81.4 us -> 76.9 us (0.945)
  Pallas kernels: 79.7 us -> 75.2 us
    pallas_call x1, Pallas kernels: 79.7 us -> 75.2 us  [on_device(): pl.pallas_call(kernel, out_shape=jax.ShapeDtypeStruct((256, 128), BF16),...]
where the time goes in v3:
time: 76.9 us; the launch traced here: 76.7 us
  Pallas kernels  75.2 us (98%)
  local copies, waits for them, and re-layouts  1.47 us (2%)
    pallas_call x1, Pallas kernels, on_device(): pl.pallas_call(kernel, out_shape=jax.ShapeDtypeStruct((256, 128), BF16),...  75.2 us

profile of v3, /device:TPU:2, one launch (start us, length us, event | category | flops | bytes accessed | tf_op | source)
XLA Modules:
  0.0 76.7 jit_solution(8459112212856553462)
XLA Ops:
  0.0 75.2 %shard_map.73 = bf16[256,128]{1,0:T(8,128)(2,1)} custom-call(bf16[1,256,128]{2,1,0:T(8,128)(2,1)} %states_hbm.1, s32[1,256]{1,0:T(1,128)} %map_hbm.1, bf16[128,4096]{1,0:T(8,128)(2,1)} %lift_hbm.1, bf16[256,256]{1,0:T(8,128)(2,1)} %gate_hbm.1, bf16[256,256]{1,0:T(8,128)(2,1)} %up_hbm.1, bf16[256,256]{1,0:T(8,128)(2,1)} %down_hbm.1, ...), custom_call_target="tpu_custom_call" | custom-call | tf_op jit(solution)/shard_map/pallas_call | solution.py:439
  75.3 1.5 %copy.9 = bf16[1,256,128]{2,1,0:T(8,128)(2,1)} copy(bf16[1,256,128]{2,1,0:T(8,128)(2,1)} %bitcast.3) | data formatting | bytes 131072

commit v4 on v3

--- a/solution.py
+++ b/solution.py
@@ -20,8 +20,8 @@
 
 def kernel(
     states_hbm, map_hbm, lift_hbm, gate_hbm, up_hbm, down_hbm, ret_hbm, out_ref,
-    slots, states_vmem, onehot_t, lift, weights, lift_out, lift_sum, lift_in, patch, acc,
-    down, ret, ret_rows, dr_half, dr_in, dr, part, half_in, pair_out, pair_in, back_out, back_in, sq_out, sq_in,
+    slots, states_vmem, onehot_t, lift, weights, lift_out, lift_far, lift_sum, lift_in, patch, acc,
+    down, ret, ret_rows, dr_half, dr_in, dr, part, part_in, back_out, back_in, sq_out, sq_in,
     load_sem,
     y_sends, y_recvs,
     sib_sends, sib_recvs,
@@ -35,7 +35,6 @@
     dg_sends, dg_recvs,
     dh_sends, dh_recvs,
     h_sends, h_recvs,
-    p_sends, p_recvs,
     b_sends, b_recvs,
     q_sends, q_recvs,
 ):
@@ -60,7 +59,6 @@
     dg_sems = (dg_sends, dg_recvs)
     dh_sems = (dh_sends, dh_recvs)
     h_sems = (h_sends, h_recvs)
-    p_sems = (p_sends, p_recvs)
     b_sems = (b_sends, b_recvs)
     q_sems = (q_sends, q_recvs)
 
@@ -162,41 +160,40 @@
     pooled = (sums / jnp.maximum(counts, 1.0)).astype(BF16)
     loads[2].wait()
 
-    def lift_go(way, hop):
-        device = {"tp": z_at(1 if way == 0 else -1)}
-        if hop == 0:
-            rows = pl.ds(32 * way, 32)
-            send(lift_out.at[4, rows], lift_in.at[way, 0, rows], lift_sems, (way, 0), device)
-        else:
-            send(lift_sum.at[way, hop], lift_in.at[way, hop], lift_sems, (way, hop), device)
-
-    def lift_arrived(way, hop):
-        rows = pl.ds(32 * way, 32) if hop == 0 else pl.ds(0, 64)
-        arrived(lift_in.at[way, hop, rows], lift_sems, (way, hop), {"tp": z_at(1)})
-
-    def lift_step(hop):
-        for way in (0, 1):
-            lift_arrived(way, hop)
-            d = 3 - hop if way == 0 else 5 + hop
-            if hop == 0:
-                rows = pl.ds(32 * way, 32)
-                rest = pl.ds(32 * (1 - way), 32)
-                lift_sum[way, 1, rest] = lift_out[d, rest]
-                lift_sum[way, 1, rows] = (
-                    lift_out[d, rows].astype(F32) + lift_in[way, 0, rows].astype(F32)
-                ).astype(BF16)
-            else:
-                lift_sum[way, hop + 1] = (
-                    lift_out[d].astype(F32) + lift_in[way, hop].astype(F32)
-                ).astype(BF16)
-            lift_go(way, hop + 1)
-
-    for d in (4, 3, 5, 2, 6, 1, 7, 0):
+    def toward(way, d):
+        return {"tp": z_at(d if way == 0 else -d)}
+
+    def lift_go(way):
+        sign = 1 if way == 0 else -1
+        rows = pl.ds(32 * way, 32)
+        send(lift_out.at[4, rows], lift_far.at[way], lift_sems, (way, 0), toward(way, 2))
+        send(lift_out.at[3 * sign % 8], lift_in.at[way, 0], lift_sems, (way, 1), toward(way, 1))
+
+    def lift_near(way):
+        sign = 1 if way == 0 else -1
+        send(lift_out.at[sign % 8], lift_in.at[way, 1], lift_sems, (way, 2), toward(way, 1))
+
+    def lift_mid():
+        for way in (0, 1):
+            sign = 1 if way == 0 else -1
+            arrived(lift_far.at[way], lift_sems, (way, 0), toward(way, 2))
+            arrived(lift_in.at[way, 0], lift_sems, (way, 1), toward(way, 1))
+            total = lift_out[2 * sign % 8].astype(F32) + lift_in[way, 0].astype(F32)
+            far = lift_far[way].astype(F32)
+            zero = jnp.zeros((32, 512), F32)
+            far = jnp.concatenate([far, zero] if way == 0 else [zero, far], axis=0)
+            lift_sum[way] = (total + far).astype(BF16)
+            send(lift_sum.at[way], lift_in.at[way, 2], lift_sems, (way, 3), toward(way, 2))
+
+    for d in (4, 3, 5, 1, 7, 2, 6, 0):
         columns = lift[:, pl.ds(pl.multiple_of(512 * z_at(d), 512), 512)]
         lift_out[d] = dot(pooled, columns).astype(BF16)
-        if d == 4:
-            lift_go(0, 0)
-            lift_go(1, 0)
+        if d == 5:
+            lift_go(0)
+            lift_go(1)
+        if d == 7:
+            lift_near(0)
+            lift_near(1)
     onehot_t[...] = jnp.transpose(onehot).astype(BF16)
     for load in loads[3:]:
         load.wait()
@@ -249,18 +246,6 @@
             arrived(dr.at[mine, units(-q)], dg_sems, (q,), {"seq": slot(q)})
         send(dr.at[mine], dr.at[mine], dh_sems, (0,), {"seq": sib})
 
-    def ring_places(way, hop):
-        return (hop, hop + 1) if way == 0 else ((8 - hop) % 8, 7 - hop)
-
-    def za_ref(e, way, hop):
-        rows = pl.ds(0, 64) if hop < 3 else pl.ds(32 * way, 32)
-        return patch.at[e, 0, rows]
-
-    def za_go(way, hop):
-        e, e2 = ring_places(way, hop)
-        send(za_ref(e, way, hop), za_ref(e2, way, hop), za_sems, (way, hop),
-             {"tp": z_at(1 if way == 0 else -1)})
-
     def first_second(i):
         return ((xa, 1), (xb, 3)) if i % 2 == 0 else ((xb, 3), (xa, 1))
 
@@ -282,49 +267,64 @@
         arrived(patch.at[e, j2], xg_sems, (e, 1), {"grp": n2})
         arrived(patch.at[e, 2], xg_sems, (e, 2), {"grp": n2})
 
-    def za_step(hop):
-        for way in (0, 1):
-            e2 = ring_places(way, hop)[1]
-            arrived(za_ref(e2, way, hop), za_sems, (way, hop), {"tp": z_at(1)})
-            if hop < 3:
-                za_go(way, hop + 1)
-                xg_one(2 * hop + 1 + way)
-        if hop == 3:
-            xg_one(7)
+    def za_near():
+        for way in (0, 1):
+            e = 1 if way == 0 else 7
+            arrived(patch.at[e, 0], za_sems, (way, 0), toward(way, 1))
+            xg_one(1 + way)
+
+    def za_mid():
+        for way in (0, 1):
+            e, e3 = ((2, 3), (6, 5))[way]
+            rows = pl.ds(32 * way, 32)
+            arrived(patch.at[e, 0], za_sems, (way, 1), toward(way, 2))
+            send(patch.at[e, 0, rows], patch.at[4, 0, rows], za_sems, (way, 3), toward(way, 2))
+            send(patch.at[e, 0], patch.at[e3, 0], za_sems, (way, 2), toward(way, 1))
+            xg_one(3 + way)
+
+    def za_far():
+        for way in (0, 1):
+            arrived(patch.at[3 if way == 0 else 5, 0], za_sems, (way, 2), toward(way, 1))
+            xg_one(5 + way)
+        for way in (0, 1):
+            rows = pl.ds(32 * way, 32)
+            arrived(patch.at[4, 0, rows], za_sems, (way, 3), toward(way, 2))
+        xg_one(7)
 
     def patch_start():
         block = lift_out[0].astype(F32)
         for way in (0, 1):
-            lift_arrived(way, 3)
-            block = block + lift_in[way, 3].astype(F32)
+            arrived(lift_in.at[way, 1], lift_sems, (way, 2), toward(way, 1))
+            arrived(lift_in.at[way, 2], lift_sems, (way, 3), toward(way, 2))
+            block = block + lift_in[way, 1].astype(F32) + lift_in[way, 2].astype(F32)
         patch[0, 0] = block.astype(BF16)
-        za_go(0, 0)
-        za_go(1, 0)
+        for way in (0, 1):
+            for d in (2, 1):
+                e = d if way == 0 else 8 - d
+                send(patch.at[0, 0], patch.at[e, 0], za_sems, (way, d - 1), toward(way, d))
         xg_one(0)
 
-    lift_step(0)
     ret_x()
-    lift_step(1)
+    lift_mid()
     y_step(0)
-    lift_step(2)
+    patch_start()
     dr_products()
-    patch_start()
+    za_near()
+    za_mid()
+    xg_two(0)
     y_step(1)
-    za_step(0)
-    xg_two(0)
-    za_step(1)
     xg_two(1)
     xg_two(2)
-    za_step(2)
-    y_step(2)
+    za_far()
     xg_two(3)
     xg_two(4)
-    za_step(3)
     dr_total()
+    y_step(2)
     xg_two(5)
     xg_two(6)
+    xg_two(7)
+    dr_share()
     y_step(3)
-    xg_two(7)
 
     squares = jnp.zeros((256, 1), F32)
     returned = jnp.zeros((64, 128), F32)
@@ -346,10 +346,7 @@
         return squares, returned
 
     sib_wait()
-    for i in range(6):
-        squares, returned = multiply(i, squares, returned)
-    dr_share()
-    for i in range(6, 8):
+    for i in range(8):
         squares, returned = multiply(i, squares, returned)
 
     scale = lax.rsqrt(squares * (1.0 / 4096) + EPS)
@@ -361,41 +358,29 @@
 
     def down_one(i):
         for n in (0, 1):
-            part[i, n] = dot(hidden, dr[2 * i + n]).astype(BF16).reshape(4, 64, 128)
-        (n1, j1), _ = first_second(i)
-        src = part.at[i, :, pl.ds(1 if j1 == 1 else 2, 2)]
-        send(src, half_in.at[i], h_sems, (i,), {"grp": n1})
+            part[i, :, n] = dot(hidden, dr[2 * i + n]).astype(BF16).reshape(4, 64, 128)
+        for j, n in ((2, (x + 2) % 4), (1, xa), (3, xb)):
+            send(part.at[i, j], part_in.at[i, j], h_sems, (i, j), {"grp": n})
 
     def down_two(i):
-        (n1, j1), (n2, j2) = first_second(i)
-        arrived(half_in.at[i], h_sems, (i,), {"grp": n1})
-        row = 1 if j1 == 1 else 0
-        pair_out[i] = (part[i, :, j2].astype(F32) + half_in[i, :, row].astype(F32)).astype(BF16)
-        send(pair_out.at[i], pair_in.at[i], p_sems, (i,), {"grp": n2})
-
-    def down_three(i):
-        (n1, j1), (n2, j2) = first_second(i)
-        arrived(pair_in.at[i], p_sems, (i,), {"grp": n2})
-        row = 0 if j1 == 1 else 1
+        total = part[i, 0].astype(F32)
+        for j in (1, 3, 2):
+            arrived(part_in.at[i, j], h_sems, (i, j), {"grp": xa})
+            total = total + part_in[i, j].astype(F32)
         for n in (0, 1):
-            total = part[i, n, 0].astype(F32) + half_in[i, n, row].astype(F32)
-            total = total + pair_in[i, n].astype(F32)
             d = 2 * i + n
             if d == 0:
-                own_total.append(total)
+                own_total.append(total[n])
             else:
-                back_out[d] = total.astype(BF16)
+                back_out[d] = total[n].astype(BF16)
                 send(back_out.at[d], back_in.at[d], b_sems, (d,), {"tp": z_at(-d)})
 
     own_total = []
     order = (2, 1, 3, 0)
     for i in order:
         down_one(i)
-    for n in range(5):
-        if n < 4:
-            down_two(order[n])
-        if n > 0:
-            down_three(order[n - 1])
+    for i in order:
+        down_two(i)
 
     returned = returned + own_total[0]
     for d in (1, 7, 2, 6, 3, 5, 4):
@@ -448,8 +433,9 @@
             pltpu.VMEM((128, 4096), BF16),
             pltpu.VMEM((16, 2, 256, 256), BF16),
             pltpu.VMEM((8, 64, 512), BF16),
-            pltpu.VMEM((2, 4, 64, 512), BF16),
-            pltpu.VMEM((2, 4, 64, 512), BF16),
+            pltpu.VMEM((2, 32, 512), BF16),
+            pltpu.VMEM((2, 64, 512), BF16),
+            pltpu.VMEM((2, 3, 64, 512), BF16),
             pltpu.VMEM((8, 4, 64, 512), BF16),
             pltpu.VMEM((2, 256, 256), F32),
             pltpu.VMEM((2, 256, 256), BF16),
@@ -458,10 +444,8 @@
             pltpu.VMEM((4, 256, 128), BF16),
             pltpu.VMEM((8, 4, 32, 128), BF16),
             pltpu.VMEM((8, 256, 128), BF16),
-            pltpu.VMEM((4, 2, 4, 64, 128), BF16),
-            pltpu.VMEM((4, 2, 2, 64, 128), BF16),
-            pltpu.VMEM((4, 2, 64, 128), BF16),
-            pltpu.VMEM((4, 2, 64, 128), BF16),
+            pltpu.VMEM((4, 4, 2, 64, 128), BF16),
+            pltpu.VMEM((4, 4, 2, 64, 128), BF16),
             pltpu.VMEM((8, 64, 128), BF16),
             pltpu.VMEM((8, 64, 128), BF16),
             pltpu.VMEM((8, 256), F32),
@@ -478,8 +462,7 @@
             dma((8,)), dma((8,)),
             dma((8,)), dma((8,)),
             dma((1,)), dma((1,)),
-            dma((4,)), dma((4,)),
-            dma((4,)), dma((4,)),
+            dma((4, 4)), dma((4, 4)),
             dma((8,)), dma((8,)),
             dma((8,)), dma((8,)),
         ],

time: 76.9 us -> 73.6 us (0.957)
  Pallas kernels: 75.2 us -> 72 us
    pallas_call x1, Pallas kernels: 75.2 us -> 72 us  [on_device(): pl.pallas_call(kernel, out_shape=jax.ShapeDtypeStruct((256, 128), BF16),...]
where the time goes in v4:
time: 73.6 us; the launch traced here: 73.4 us
  Pallas kernels  72 us (98%)
  local copies, waits for them, and re-layouts  1.47 us (2%)
    pallas_call x1, Pallas kernels, on_device(): pl.pallas_call(kernel, out_shape=jax.ShapeDtypeStruct((256, 128), BF16),...  72 us
    unnamed x1, local copies, waits for them, and re-layouts  1.47 us

profile of v4, /device:TPU:2, one launch (start us, length us, event | category | flops | bytes accessed | tf_op | source)
XLA Modules:
  0.0 73.4 jit_solution(10815420515095168653)
XLA Ops:
  0.0 72.0 %shard_map.73 = bf16[256,128]{1,0:T(8,128)(2,1)} custom-call(bf16[1,256,128]{2,1,0:T(8,128)(2,1)} %states_hbm.1, s32[1,256]{1,0:T(1,128)} %map_hbm.1, bf16[128,4096]{1,0:T(8,128)(2,1)} %lift_hbm.1, bf16[256,256]{1,0:T(8,128)(2,1)} %gate_hbm.1, bf16[256,256]{1,0:T(8,128)(2,1)} %up_hbm.1, bf16[256,256]{1,0:T(8,128)(2,1)} %down_hbm.1, ...), custom_call_target="tpu_custom_call" | custom-call | tf_op jit(solution)/shard_map/pallas_call | solution.py:424
  72.0 1.5 %copy.9 = bf16[1,256,128]{2,1,0:T(8,128)(2,1)} copy(bf16[1,256,128]{2,1,0:T(8,128)(2,1)} %bitcast.3) | data formatting | bytes 131072

commit v5 on v4

--- a/solution.py
+++ b/solution.py
@@ -21,7 +21,7 @@
 def kernel(
     states_hbm, map_hbm, lift_hbm, gate_hbm, up_hbm, down_hbm, ret_hbm, out_ref,
     slots, states_vmem, onehot_t, lift, weights, lift_out, lift_far, lift_sum, lift_in, patch, acc,
-    down, ret, ret_rows, dr_half, dr_in, dr, part, part_in, back_out, back_in, sq_out, sq_in,
+    down, ret, ret_rows, dr_half, dr_far, dr_sum, dr_in, dr, part, part_in, back_out, back_in, sq_out, sq_in,
     load_sem,
     y_sends, y_recvs,
     sib_sends, sib_recvs,
@@ -94,7 +94,7 @@
     for load in loads:
         load.start()
     barrier = pltpu.get_barrier_semaphore()
-    partners = [{"seq": slot(d)} for d in range(1, 8)] + [{"seq": sib}]
+    partners = [{"seq": slot(d)} for d in (1, -1, 2, -2)] + [{"seq": sib}]
     partners += [{"grp": xa}, {"grp": xb}, {"grp": (x + 2) % 4}]
     partners += [{"tp": z_at(d)} for d in range(1, 8)]
     for partner in partners:
@@ -220,6 +220,12 @@
     def units(q):
         return pl.ds(32 * ((y + q + 8) % 8), 32)
 
+    def far_units(way, q):
+        return pl.ds(32 * ((y + q + 8) % 8) + 16 * way, 16)
+
+    def along(way, d):
+        return {"seq": slot(d if way == 0 else -d)}
+
     def dr_products():
         for j in (1, 3, 2):
             arrived(ret_rows.at[:, :, x], rx_sems, (j,), {"grp": xa})
@@ -228,22 +234,50 @@
             val = dot(down[0], ret_rows[k, 0].reshape(256, 128))
             val = val + dot(down[1], ret_rows[k, 1].reshape(256, 128))
             dr_half[k] = val.astype(BF16)
-        for q in (4, 3, 5, 2, 6, 1, 7):
-            send(dr_half.at[:, units(q)], dr_in.at[q], dy_sems, (q,), {"seq": slot(q)})
+        for way in (0, 1):
+            sign = 1 if way == 0 else -1
+            send(dr_half.at[:, far_units(way, 4)], dr_far.at[way], dy_sems, (way, 0), along(way, 2))
+            send(dr_half.at[:, units(3 * sign)], dr_in.at[way, 0], dy_sems, (way, 1), along(way, 1))
+            send(dr_half.at[:, units(sign)], dr_in.at[way, 1], dy_sems, (way, 2), along(way, 1))
+
+    def dr_mid():
+        for way in (0, 1):
+            sign = 1 if way == 0 else -1
+            arrived(dr_far.at[way], dy_sems, (way, 0), along(way, 2))
+            arrived(dr_in.at[way, 0], dy_sems, (way, 1), along(way, 1))
+            total = dr_half[:, units(2 * sign)].astype(F32) + dr_in[way, 0].astype(F32)
+            far = dr_far[way].astype(F32)
+            zero = jnp.zeros((4, 16, 128), F32)
+            far = jnp.concatenate([far, zero] if way == 0 else [zero, far], axis=1)
+            dr_sum[way] = (total + far).astype(BF16)
+            send(dr_sum.at[way], dr_in.at[way, 2], dy_sems, (way, 3), along(way, 2))
 
     def dr_total():
         total = dr_half[:, units(0)].astype(F32)
-        for q in (1, 7, 2, 6, 3, 5, 4):
-            arrived(dr_in.at[q], dy_sems, (q,), {"seq": slot(q)})
-            total = total + dr_in[q].astype(F32)
+        for way in (0, 1):
+            arrived(dr_in.at[way, 1], dy_sems, (way, 2), along(way, 1))
+            arrived(dr_in.at[way, 2], dy_sems, (way, 3), along(way, 2))
+            total = total + dr_in[way, 1].astype(F32) + dr_in[way, 2].astype(F32)
         dr[mine, units(0)] = total.astype(BF16)
-        for q in (4, 3, 5, 2, 6, 1, 7):
+        for way in (0, 1):
             ref = dr.at[mine, units(0)]
-            send(ref, ref, dg_sems, (q,), {"seq": slot(q)})
+            for d in (2, 1):
+                send(ref, ref, dg_sems, (way, d - 1), along(way, d))
+
+    def dr_pass():
+        for way in (0, 1):
+            ref = dr.at[mine, units(-2 if way == 0 else 2)]
+            arrived(ref, dg_sems, (way, 1), along(way, 2))
+            half = dr.at[mine, far_units(way, -2 if way == 0 else 2)]
+            send(half, half, dg_sems, (way, 3), along(way, 2))
+            send(ref, ref, dg_sems, (way, 2), along(way, 1))
 
     def dr_share():
-        for q in (1, 7, 2, 6, 3, 5, 4):
-            arrived(dr.at[mine, units(-q)], dg_sems, (q,), {"seq": slot(q)})
+        for way in (0, 1):
+            sign = 1 if way == 0 else -1
+            arrived(dr.at[mine, units(-sign)], dg_sems, (way, 0), along(way, 1))
+            arrived(dr.at[mine, units(-3 * sign)], dg_sems, (way, 2), along(way, 1))
+            arrived(dr.at[mine, far_units(way, 4)], dg_sems, (way, 3), along(way, 2))
         send(dr.at[mine], dr.at[mine], dh_sems, (0,), {"seq": sib})
 
     def first_second(i):
@@ -312,18 +346,19 @@
     za_near()
     za_mid()
     xg_two(0)
+    dr_mid()
     y_step(1)
     xg_two(1)
     xg_two(2)
     za_far()
+    dr_total()
     xg_two(3)
     xg_two(4)
-    dr_total()
     y_step(2)
+    dr_pass()
     xg_two(5)
     xg_two(6)
     xg_two(7)
-    dr_share()
     y_step(3)
 
     squares = jnp.zeros((256, 1), F32)
@@ -346,7 +381,10 @@
         return squares, returned
 
     sib_wait()
-    for i in range(8):
+    for i in range(6):
+        squares, returned = multiply(i, squares, returned)
+    dr_share()
+    for i in range(6, 8):
         squares, returned = multiply(i, squares, returned)
 
     scale = lax.rsqrt(squares * (1.0 / 4096) + EPS)
@@ -442,7 +480,9 @@
             pltpu.VMEM((8, 2, 4, 64, 128), BF16),
             pltpu.VMEM((4, 2, 4, 64, 128), BF16),
             pltpu.VMEM((4, 256, 128), BF16),
-            pltpu.VMEM((8, 4, 32, 128), BF16),
+            pltpu.VMEM((2, 4, 16, 128), BF16),
+            pltpu.VMEM((2, 4, 32, 128), BF16),
+            pltpu.VMEM((2, 3, 4, 32, 128), BF16),
             pltpu.VMEM((8, 256, 128), BF16),
             pltpu.VMEM((4, 4, 2, 64, 128), BF16),
             pltpu.VMEM((4, 4, 2, 64, 128), BF16),
@@ -459,8 +499,8 @@
             dma((4,)), dma((4,)),
             dma((4,)), dma((4,)),
             dma((1,)), dma((1,)),
-            dma((8,)), dma((8,)),
-            dma((8,)), dma((8,)),
+            dma((2, 4)), dma((2, 4)),
+            dma((2, 4)), dma((2, 4)),
             dma((1,)), dma((1,)),
             dma((4, 4)), dma((4, 4)),
             dma((8,)), dma((8,)),

time: 73.6 us -> 72.8 us (0.989)
  Pallas kernels: 72 us -> 71.1 us
    pallas_call x1, Pallas kernels: 72 us -> 71.1 us  [on_device(): pl.pallas_call(kernel, out_shape=jax.ShapeDtypeStruct((256, 128), BF16),...]
where the time goes in v5:
time: 72.8 us; the launch traced here: 72.5 us
  Pallas kernels  71.1 us (98%)
  local copies, waits for them, and re-layouts  1.47 us (2%)
    pallas_call x1, Pallas kernels, on_device(): pl.pallas_call(kernel, out_shape=jax.ShapeDtypeStruct((256, 128), BF16),...  71.1 us
    unnamed x1, local copies, waits for them, and re-layouts  1.47 us

profile of v5, /device:TPU:2, one launch (start us, length us, event | category | flops | bytes accessed | tf_op | source)
XLA Modules:
  0.0 72.5 jit_solution(17018223375595941683)
XLA Ops:
  0.0 71.1 %shard_map.73 = bf16[256,128]{1,0:T(8,128)(2,1)} custom-call(bf16[1,256,128]{2,1,0:T(8,128)(2,1)} %states_hbm.1, s32[1,256]{1,0:T(1,128)} %map_hbm.1, bf16[128,4096]{1,0:T(8,128)(2,1)} %lift_hbm.1, bf16[256,256]{1,0:T(8,128)(2,1)} %gate_hbm.1, bf16[256,256]{1,0:T(8,128)(2,1)} %up_hbm.1, bf16[256,256]{1,0:T(8,128)(2,1)} %down_hbm.1, ...), custom_call_target="tpu_custom_call" | custom-call | tf_op jit(solution)/shard_map/pallas_call | solution.py:462
  71.1 1.5 %copy.9 = bf16[1,256,128]{2,1,0:T(8,128)(2,1)} copy(bf16[1,256,128]{2,1,0:T(8,128)(2,1)} %bitcast.3) | data formatting | bytes 131072

commit v6 on v5

--- a/solution.py
+++ b/solution.py
@@ -362,14 +362,12 @@
     y_step(3)
 
     squares = jnp.zeros((256, 1), F32)
-    returned = jnp.zeros((64, 128), F32)
-
-    def multiply(i, squares, returned):
+
+    def multiply(i, squares):
         xg_wait(i)
         e = IN_ORDER[i]
         kb = z_at(-e)
         rows = patch[e].reshape(256, 512)
-        returned = returned + dot(patch[e, 0], ret[kb].reshape(512, 128))
         wide = rows.astype(F32)
         squares = squares + jnp.sum(wide * wide, axis=1, keepdims=True)
         for a in (0, 1):
@@ -378,14 +376,14 @@
                 acc[a] = dot(rows, w)
             else:
                 acc[a] += dot(rows, w)
-        return squares, returned
+        return squares
 
     sib_wait()
     for i in range(6):
-        squares, returned = multiply(i, squares, returned)
+        squares = multiply(i, squares)
     dr_share()
     for i in range(6, 8):
-        squares, returned = multiply(i, squares, returned)
+        squares = multiply(i, squares)
 
     scale = lax.rsqrt(squares * (1.0 / 4096) + EPS)
     gate = acc[0] * scale
@@ -417,6 +415,9 @@
     order = (2, 1, 3, 0)
     for i in order:
         down_one(i)
+    returned = jnp.zeros((64, 128), F32)
+    for e in range(8):
+        returned = returned + dot(patch[e, 0], ret[z_at(-e)].reshape(512, 128))
     for i in order:
         down_two(i)
 

time: 72.8 us -> 72.8 us (level)
  the two profiles are of different devices: /device:TPU:2 before, /device:TPU:16 now
where the time goes in v6:
time: 72.8 us; the launch traced here: 72.6 us
  Pallas kernels  71.1 us (98%)
  local copies, waits for them, and re-layouts  1.47 us (2%)
    pallas_call x1, Pallas kernels, on_device(): pl.pallas_call(kernel, out_shape=jax.ShapeDtypeStruct((256, 128), BF16),...  71.1 us
    unnamed x1, local copies, waits for them, and re-layouts  1.47 us

profile of v6, /device:TPU:16, one launch (start us, length us, event | category | flops | bytes accessed | tf_op | source)
XLA Modules:
  0.0 72.6 jit_solution(17910375884709381895)
XLA Ops:
  0.0 71.1 %shard_map.73 = bf16[256,128]{1,0:T(8,128)(2,1)} custom-call(bf16[1,256,128]{2,1,0:T(8,128)(2,1)} %states_hbm.1, s32[1,256]{1,0:T(1,128)} %map_hbm.1, bf16[128,4096]{1,0:T(8,128)(2,1)} %lift_hbm.1, bf16[256,256]{1,0:T(8,128)(2,1)} %gate_hbm.1, bf16[256,256]{1,0:T(8,128)(2,1)} %up_hbm.1, bf16[256,256]{1,0:T(8,128)(2,1)} %down_hbm.1, ...), custom_call_target="tpu_custom_call" | custom-call | tf_op jit(solution)/shard_map/pallas_call | solution.py:463
  71.2 1.5 %copy.9 = bf16[1,256,128]{2,1,0:T(8,128)(2,1)} copy(bf16[1,256,128]{2,1,0:T(8,128)(2,1)} %bitcast.3) | data formatting | bytes 131072
